TPU v7x, 128 devices: a whole 4x4x4 slice. The times are simulated.
128 devices in a mesh: seq: 16 (over x_hi, y, core), head: 8 (over z, x_lo).
Axes of the slice: x: 4 (x_hi: 2, x_lo: 2; x = x_hi * 2 + x_lo), y: 4, z: 4, core: 2. Of those that a mesh axis runs over, the one named last changes fastest.
Arguments:
- prompt_k: bfloat16 [5120, 1024], P(('seq', 'head')), may hold values from -6 to 6
- prompt_v: bfloat16 [5120, 1024], P(('seq', 'head')), may hold values from -6 to 6
- resp_q: bfloat16 [4096, 8192], P('seq', 'head'), may hold values from -7 to 7
- resp_k: bfloat16 [4096, 1024], P('seq', 'head'), may hold values from -6 to 6
- resp_v: bfloat16 [4096, 1024], P('seq', 'head'), may hold values from -6 to 6
- grad_out: bfloat16 [4096, 8192], P('seq', 'head'), may hold values from -6 to 6
- resp_lengths: int32 [8], replicated, may hold values from 1 to 1024, 4096 in all
Outputs:
- resp_out: bfloat16 [4096, 8192], P('seq', 'head')
- grad_q: bfloat16 [4096, 8192], P('seq', 'head')
- grad_k_resp: bfloat16 [4096, 1024], P('seq', 'head')
- grad_v_resp: bfloat16 [4096, 1024], P('seq', 'head')
- grad_k_prompt: bfloat16 [5120, 1024], P(('seq', 'head'))
- grad_v_prompt: bfloat16 [5120, 1024], P(('seq', 'head'))
Inputs may be any that keep to these rules, and one draw needn't show every extreme that they name: `resp_lengths`: the 8 lengths add up to 4096, and the largest is exactly 1024.
All inputs are finite; a program needn't handle non-finite values.
Results may differ from a plain program's by a relative error of at most 0.02.
Values may be sent and summed in bfloat16 or wider, within the bound.
A program may use at most 128 MiB of HBM per device.

v0:
```python
import math

import jax
import jax.numpy as jnp
from jax import lax
from jax.sharding import PartitionSpec as P

HD = 128
SPAN = 4


neg_large = -1e30


def passed_along(array, axis, by):
    devices = lax.axis_size(axis)
    pairs = [(i, i + by) for i in range(devices) if 0 <= i + by < devices]
    return lax.ppermute(array, axis, pairs)


def segment_of(positions, seg_ends):
    return jnp.sum((positions[:, None] >= seg_ends[None, :]).astype(jnp.int32), axis=1)


def block_count(length):
    pieces = max(1, length // 512)
    while length % pieces != 0:
        pieces = pieces - 1
    return pieces


def masked_scores(queries, key_rows, allowed, score_scale):
    scores = (
        jnp.einsum("qngd,knd->qngk", queries, key_rows, preferred_element_type=jnp.float32)
        * score_scale
    )
    if allowed is None:
        return scores
    return jnp.where(allowed[:, None, None, :], scores, neg_large)


def block_stats(queries, key_rows, allowed, score_scale):
    scores = masked_scores(queries, key_rows, allowed, score_scale)
    row_max = jnp.max(scores, axis=-1)
    row_total = jnp.sum(jnp.exp(scores - row_max[..., None]), axis=-1)
    return (row_max, row_total)


def merge_stats(earlier, later):
    row_max = jnp.maximum(earlier[0], later[0])
    row_total = earlier[1] * jnp.exp(earlier[0] - row_max) + later[1] * jnp.exp(later[0] - row_max)
    return (row_max, row_total)


def block_output(queries, key_rows, values, allowed, log_total, score_scale):
    weights = jnp.exp(masked_scores(queries, key_rows, allowed, score_scale) - log_total[..., None])
    return jnp.einsum(
        "qngk,knd->qngd", weights.astype(jnp.bfloat16), values, preferred_element_type=jnp.float32
    )


def block_backward(
    queries, cotangent, key_rows, values, allowed, log_total, row_delta, score_scale
):
    weights = jnp.exp(masked_scores(queries, key_rows, allowed, score_scale) - log_total[..., None])
    rounded = weights.astype(jnp.bfloat16)
    grad_prob = jnp.einsum("qngd,knd->qngk", cotangent, values, preferred_element_type=jnp.float32)
    dscore = (weights * (grad_prob - row_delta[..., None]) * score_scale).astype(jnp.bfloat16)
    return (rounded, dscore)


def grad_query_of(dscore, key_rows):
    return jnp.einsum("qngk,knd->qngd", dscore, key_rows, preferred_element_type=jnp.float32)


def grad_kv_of(rounded, dscore, queries, cotangent):
    grad_key = jnp.einsum("qngk,qngd->knd", dscore, queries, preferred_element_type=jnp.float32)
    grad_value = jnp.einsum(
        "qngk,qngd->knd", rounded, cotangent, preferred_element_type=jnp.float32
    )
    return (grad_key, grad_value)


def shards(prompt_k, prompt_v, resp_q, resp_k, resp_v, grad_out, resp_lengths):
    kv_cols = resp_k.shape[1]
    kv_heads = kv_cols // HD
    q_heads = resp_q.shape[1] // HD
    group_size = q_heads // kv_heads
    row_count = resp_q.shape[0]
    seq_devices = lax.axis_size("seq")
    head_devices = lax.axis_size("head")
    score_scale = 1.0 / math.sqrt(HD)
    queries = resp_q.reshape(row_count, kv_heads, group_size, HD)
    cotangent = grad_out.reshape(row_count, kv_heads, group_size, HD)
    seg_ends = jnp.cumsum(resp_lengths)
    first_row = lax.axis_index("seq") * row_count
    row_pos = first_row + jnp.arange(row_count, dtype=jnp.int32)
    row_seg = segment_of(row_pos, seg_ends)
    block_rows = prompt_k.shape[0]
    rows_k, rows_v = (
        lax.all_gather(prompt_k, "seq", axis=0, tiled=True),
        lax.all_gather(prompt_v, "seq", axis=0, tiled=True),
    )
    cols_k, cols_v = (
        lax.all_to_all(rows_k, "head", split_axis=1, concat_axis=0, tiled=True),
        lax.all_to_all(rows_v, "head", split_axis=1, concat_axis=0, tiled=True),
    )
    prompt_keys = (
        cols_k.reshape(head_devices, seq_devices, block_rows, kv_cols)
        .transpose(1, 0, 2, 3)
        .reshape(head_devices * seq_devices * block_rows, kv_cols)
    )
    prompt_values = (
        cols_v.reshape(head_devices, seq_devices, block_rows, kv_cols)
        .transpose(1, 0, 2, 3)
        .reshape(head_devices * seq_devices * block_rows, kv_cols)
    )
    prompt_len = prompt_keys.shape[0]
    key_blocks = block_count(prompt_len)
    key_block = prompt_len // key_blocks
    prompt_key_blocks = prompt_keys.reshape(key_blocks, key_block, kv_heads, HD)
    prompt_value_blocks = prompt_values.reshape(key_blocks, key_block, kv_heads, HD)

    def allowed_for(distance):
        key_pos = first_row - distance * row_count + jnp.arange(row_count, dtype=jnp.int32)
        key_seg = segment_of(key_pos, seg_ends)
        return (
            (key_pos[None, :] >= 0)
            & (key_pos[None, :] <= row_pos[:, None])
            & (key_seg[None, :] == row_seg[:, None])
        )

    response_blocks = [
        (
            resp_k.reshape(row_count, kv_heads, HD),
            resp_v.reshape(row_count, kv_heads, HD),
            allowed_for(0),
        )
    ]
    for distance in range(1, SPAN + 1):
        far_k, far_v = passed_along((resp_k, resp_v), "seq", distance)
        response_blocks.append(
            (
                far_k.reshape(row_count, kv_heads, HD),
                far_v.reshape(row_count, kv_heads, HD),
                allowed_for(distance),
            )
        )
    stat_shape = (row_count, kv_heads, group_size)
    no_stats = (jnp.full(stat_shape, neg_large, jnp.float32), jnp.zeros(stat_shape, jnp.float32))

    def prompt_stats(running, key_rows):
        return (merge_stats(running, block_stats(queries, key_rows, None, score_scale)), None)

    statistics, ignored = lax.scan(prompt_stats, no_stats, prompt_key_blocks)
    for distance, (key_rows, values, allowed) in enumerate(response_blocks):

        def stats_here(key_rows=key_rows, allowed=allowed):
            return block_stats(queries, key_rows, allowed, score_scale)

        found = stats_here() if distance == 0 else stats_here()
        statistics = merge_stats(statistics, found)
    log_total = statistics[0] + jnp.log(statistics[1])
    zero_out = jnp.zeros((row_count, kv_heads, group_size, HD), jnp.float32)

    def prompt_output(running, pair_rows):
        return (
            running
            + block_output(queries, pair_rows[0], pair_rows[1], None, log_total, score_scale),
            None,
        )

    accumulated, ignored = lax.scan(
        prompt_output, zero_out, (prompt_key_blocks, prompt_value_blocks)
    )
    for distance, (key_rows, values, allowed) in enumerate(response_blocks):

        def output_here(key_rows=key_rows, values=values, allowed=allowed):
            return block_output(queries, key_rows, values, allowed, log_total, score_scale)

        accumulated = accumulated + (output_here() if distance == 0 else output_here())
    resp_out = accumulated.astype(jnp.bfloat16)
    row_delta = jnp.sum(cotangent.astype(jnp.float32) * resp_out.astype(jnp.float32), axis=-1)

    def prompt_backward(running, pair_rows):
        rounded, dscore = block_backward(
            queries, cotangent, pair_rows[0], pair_rows[1], None, log_total, row_delta, score_scale
        )
        grad_key, grad_value = grad_kv_of(rounded, dscore, queries, cotangent)
        return (running + grad_query_of(dscore, pair_rows[0]), (grad_key, grad_value))

    grad_query, (key_grads, value_grads) = lax.scan(
        prompt_backward, zero_out, (prompt_key_blocks, prompt_value_blocks)
    )
    summed_k, summed_v = (
        lax.psum_scatter(
            key_grads.reshape(prompt_len, kv_cols), "seq", scatter_dimension=0, tiled=True
        ),
        lax.psum_scatter(
            value_grads.reshape(prompt_len, kv_cols), "seq", scatter_dimension=0, tiled=True
        ),
    )
    back_k, back_v = (
        lax.all_to_all(
            summed_k.astype(jnp.bfloat16), "head", split_axis=0, concat_axis=1, tiled=True
        ),
        lax.all_to_all(
            summed_v.astype(jnp.bfloat16), "head", split_axis=0, concat_axis=1, tiled=True
        ),
    )
    own_grad_k = jnp.zeros((row_count, kv_cols), jnp.float32)
    own_grad_v = jnp.zeros((row_count, kv_cols), jnp.float32)
    for distance, (key_rows, values, allowed) in enumerate(response_blocks):

        def backward_here(key_rows=key_rows, values=values, allowed=allowed):
            rounded, dscore = block_backward(
                queries, cotangent, key_rows, values, allowed, log_total, row_delta, score_scale
            )
            grad_key, grad_value = grad_kv_of(rounded, dscore, queries, cotangent)
            return (grad_query_of(dscore, key_rows), grad_key, grad_value)

        if distance == 0:
            part_query, part_key, part_value = backward_here()
            own_grad_k = part_key.reshape(row_count, kv_cols)
            own_grad_v = part_value.reshape(row_count, kv_cols)
        else:
            part_query, part_key, part_value = backward_here()
            back_key, back_value = passed_along(
                (part_key.reshape(row_count, kv_cols), part_value.reshape(row_count, kv_cols)),
                "seq",
                -distance,
            )
            own_grad_k = own_grad_k + back_key
            own_grad_v = own_grad_v + back_value
        grad_query = grad_query + part_query
    return (
        resp_out.reshape(row_count, q_heads * HD),
        grad_query.astype(jnp.bfloat16).reshape(row_count, q_heads * HD),
        own_grad_k.astype(jnp.bfloat16),
        own_grad_v.astype(jnp.bfloat16),
        back_k,
        back_v,
    )


def solution(mesh):
    placed = (
        P(("seq", "head"), None),
        P(("seq", "head"), None),
        P("seq", "head"),
        P("seq", "head"),
        P("seq", "head"),
        P("seq", "head"),
        P(),
    )
    return jax.shard_map(
        shards,
        mesh=mesh,
        in_specs=placed,
        out_specs=(
            P("seq", "head"),
            P("seq", "head"),
            P("seq", "head"),
            P("seq", "head"),
            P(("seq", "head"), None),
            P(("seq", "head"), None),
        ),
        check_vma=False,
    )
```

profile of v0, /device:TPU:2, one launch (start us, length us, event | category | flops | bytes accessed | tf_op | source)
XLA Modules:
  0.0 468.5 jit_solution(16361576492132983653)
XLA Ops:
  10.2 5.1 %collective-permute-start.7 = (bf16[256,128]{0,1:T(8,128)(2,1)}, bf16[256,128]{0,1:T(8,128)(2,1)S(1)}, u32[]{:S(2)}, u32[]{:S(2)}) collective-permute-start(bf16[256,128]{0,1:T(8,128)(2,1)} %copy.279), channel_id=1, source_target_pairs={{0,32},{8,40},{16,48},{24,56},{32,64},{40,72},{48,80},{56,88},{64,... | collective-permute-start | bytes 196616 | tf_op jit(solution)/shard_map/ppermute | solution.py:18
  20.2 4.2 collective-permute-start.4
  28.7 29.0 %all-gather.3.cloned.1.call-done = bf16[640,1024]{1,0:T(8,128)(2,1)} async-done(((bf16[40,1024]{1,0:T(8,128)(2,1)}), bf16[640,1024]{1,0:T(8,128)(2,1)}) %all-gather.3.cloned.1.call-update) | async-done | bytes 1310736 | tf_op jit(solution)/shard_map/all_gather | solution.py:102
  60.2 5.9 %all-to-all-start = ((bf16[640,8,128]{0,2,1:T(8,128)(2,1)}), bf16[640,8,128]{0,2,1:T(8,128)(2,1)}, u32[]{:S(2)}, u32[]{:S(2)}) async-start(bf16[640,8,128]{0,2,1:T(8,128)(2,1)} %bitcast), calls=%async_computation | async-start | bytes 2621440 | tf_op jit(solution)/shard_map/all_to_all | solution.py:106
  83.0 21.8 %all-gather.5.cloned.1.call-done = bf16[640,1024]{1,0:T(8,128)(2,1)} async-done(((bf16[40,1024]{1,0:T(8,128)(2,1)}), bf16[640,1024]{1,0:T(8,128)(2,1)}) %all-gather.5.cloned.1.call-update) | async-done | bytes 1310736 | tf_op jit(solution)/shard_map/all_gather | solution.py:101
  107.2 5.9 %all-to-all-start.1 = ((bf16[640,8,128]{0,2,1:T(8,128)(2,1)}), bf16[640,8,128]{0,2,1:T(8,128)(2,1)}, u32[]{:S(2)}, u32[]{:S(2)}) async-start(bf16[640,8,128]{0,2,1:T(8,128)(2,1)} %bitcast.861), calls=%async_computation.1 | async-start | bytes 2621440 | tf_op jit(solution)/shard_map/all_to_all | solution.py:105
  115.6 3.5 collective-permute-start.3
  136.0 23.7 %while.39 = (s32[]{:T(128)}, f32[256,1,8]{0,2,1:T(8,128)S(1)}, f32[256,1,8]{0,2,1:T(8,128)S(1)}, bf16[10,512,1,128]{3,1,2,0:T(8,128)(2,1)}, bf16[256,1,8,128]{3,0,2,1:T(8,128)(2,1)S(1)}, /*index=5*/s32[]{:T(128)}, s32[]{:T(128)}) while((s32[]{:T(128)}, f32[256,1,8]{0,2,1:T(8,128)S(1)}, f32[256,1,8]{0,2,1:T(8,128)S(1)}, ...), condition=%wide.region_3.4_spmd.clone, body=%wide.region_0.3_spmd.clone.sunk | while | flops 273690624 | bytes 9117795 | solution.py:155
  160.4 34.3 %while.40 = (s32[]{:T(128)}, f32[256,1,8,128]{0,3,2,1:T(8,128)}, bf16[10,512,1,128]{3,1,0,2:T(8,128)(2,1)}, bf16[10,512,1,128]{3,1,2,0:T(8,128)(2,1)}, bf16[256,...) while((s32[]{:T(128)}, f32[256,1,8,128]{0,3,2,1:T(8,128)}, ...), condition=%wide.region_21.22_spmd.clone, body=%wide.region_20.21_spmd.clone.sunk | while | flops 540540928 | bytes 2893414 | solution.py:173
  163.5 3.5 fusion.286
  167.0 3.5 fusion.286
  170.5 3.5 fusion.286
  174.0 3.5 fusion.286
  177.4 3.5 fusion.286
  180.9 3.5 fusion.286
  184.4 3.5 fusion.286
  187.8 3.5 fusion.286
  191.3 3.5 fusion.286
  202.6 81.9 %while.41 = (s32[]{:T(128)}, f32[256,1,8,128]{0,3,2,1:T(8,128)S(1)}, f32[10,512,1,128]{3,1,2,0:T(8,128)}, f32[10,512,1,128]{3,1,2,0:T(8,128)}, bf16[10,512,1,128...) while((s32[]{:T(128)}, ...), condition=%wide.region_24.25_spmd.clone, body=%wide.region_23.24_spmd.clone.sunk | while | flops 1352138752 | bytes 24010908 | solution.py:192
  328.1 44.4 %reduce-scatter.3.cloned.1.call-done = f32[320,128]{1,0:T(8,128)} async-done(((f32[5120,128]{1,0:T(8,128)}), f32[320,128]{1,0:T(8,128)}) %reduce-scatter.3.cloned.1.call-update) | async-done | bytes 163856 | tf_op jit(solution)/shard_map/reduce_scatter | solution.py:196
  374.1 5.9 %all-to-all-start.2 = ((bf16[8,40,128]{2,1,0:T(8,128)(2,1)}), bf16[8,40,128]{2,1,0:T(8,128)(2,1)S(1)}, u32[]{:S(2)}, u32[]{:S(2)}) async-start(bf16[8,40,128]{2,1,0:T(8,128)(2,1)} %bitcast.123), calls=%async_computation.3 | async-start | bytes 163840 | tf_op jit(solution)/shard_map/all_to_all | solution.py:204
  382.4 66.4 %reduce-scatter.5.cloned.1.call-done = f32[320,128]{1,0:T(8,128)} async-done(((f32[5120,128]{1,0:T(8,128)}), f32[320,128]{1,0:T(8,128)}) %reduce-scatter.5.cloned.1.call-update) | async-done | bytes 163856 | tf_op jit(solution)/shard_map/reduce_scatter | solution.py:199
  450.3 5.9 %all-to-all-start.3 = ((bf16[8,40,128]{2,1,0:T(8,128)(2,1)}), bf16[8,40,128]{2,1,0:T(8,128)(2,1)S(1)}, u32[]{:S(2)}, u32[]{:S(2)}) async-start(bf16[8,40,128]{2,1,0:T(8,128)(2,1)} %bitcast.126), calls=%async_computation.5 | async-start | bytes 163840 | tf_op jit(solution)/shard_map/all_to_all | solution.py:207
  456.8 4.5 all-to-all-done.3
  (251 shorter events, 219.7 us)
Async XLA Ops:
  7.2 50.6 %all-gather.3.cloned.1.call-start = ((), (), s32[]{:S(2)}) async-start(), calls=%async_computation.6 | async-start | bytes 1392640 | tf_op jit(solution)/shard_map/all_gather | solution.py:102
  7.9 96.8 %all-gather.5.cloned.1.call-start = ((), (), s32[]{:S(2)}) async-start(), calls=%async_computation.7 | async-start | bytes 1392640 | tf_op jit(solution)/shard_map/all_gather | solution.py:101
  10.2 189.2 %collective-permute-start.7 = (bf16[256,128]{0,1:T(8,128)(2,1)}, bf16[256,128]{0,1:T(8,128)(2,1)S(1)}, u32[]{:S(2)}, u32[]{:S(2)}) collective-permute-start(bf16[256,128]{0,1:T(8,128)(2,1)} %copy.279), channel_id=1, source_target_pairs={{0,32},{8,40},{16,48},{24,56},{32,64},{40,72},{48,80},{56,88},{64,... | collective-permute-start | bytes 196616 | tf_op jit(solution)/shard_map/ppermute | solution.py:18
  15.3 182.5 %collective-permute-start.6 = (bf16[256,128]{0,1:T(8,128)(2,1)}, bf16[256,128]{0,1:T(8,128)(2,1)S(1)}, u32[]{:S(2)}, u32[]{:S(2)}) collective-permute-start(bf16[256,128]{0,1:T(8,128)(2,1)} %copy.279), channel_id=1, source_target_pairs={{0,24},{8,32},{16,40},{24,48},{32,56},{40,64},{48,72},{56,80},{64,... | collective-permute-start | bytes 196616 | tf_op jit(solution)/shard_map/ppermute | solution.py:18
  17.1 180.2 %collective-permute-start.5 = (bf16[256,128]{0,1:T(8,128)(2,1)}, bf16[256,128]{0,1:T(8,128)(2,1)S(1)}, u32[]{:S(2)}, u32[]{:S(2)}) collective-permute-start(bf16[256,128]{0,1:T(8,128)(2,1)} %copy.279), channel_id=1, source_target_pairs={{0,16},{8,24},{16,32},{24,40},{32,48},{40,56},{48,64},{56,72},{64,... | collective-permute-start | bytes 196616 | tf_op jit(solution)/shard_map/ppermute | solution.py:18
  20.2 180.0 %collective-permute-start.4 = (bf16[256,128]{0,1:T(8,128)(2,1)}, bf16[256,128]{0,1:T(8,128)(2,1)S(1)}, u32[]{:S(2)}, u32[]{:S(2)}) collective-permute-start(bf16[256,128]{0,1:T(8,128)(2,1)} %copy.279), channel_id=1, source_target_pairs={{0,8},{8,16},{16,24},{24,32},{32,40},{40,48},{48,56},{56,64},{64,7... | collective-permute-start | bytes 196616 | tf_op jit(solution)/shard_map/ppermute | solution.py:18
  24.4 47.7 %collective-permute-start = (bf16[256,128]{1,0:T(8,128)(2,1)}, bf16[256,128]{1,0:T(8,128)(2,1)S(1)}, u32[]{:S(2)}, u32[]{:S(2)}) collective-permute-start(bf16[256,128]{1,0:T(8,128)(2,1)} %param.16), channel_id=1, source_target_pairs={{0,8},{8,16},{16,24},{24,32},{32,40},{40,48},{48,56},{56,64},{64,7... | collective-permute-start | bytes 196616 | tf_op jit(solution)/shard_map/ppermute | solution.py:18
  60.2 47.0 %all-to-all-start = ((bf16[640,8,128]{0,2,1:T(8,128)(2,1)}), bf16[640,8,128]{0,2,1:T(8,128)(2,1)}, u32[]{:S(2)}, u32[]{:S(2)}) async-start(bf16[640,8,128]{0,2,1:T(8,128)(2,1)} %bitcast), calls=%async_computation | async-start | bytes 2621440 | tf_op jit(solution)/shard_map/all_to_all | solution.py:106
  72.1 6.2 %collective-permute-start.1 = (bf16[256,128]{1,0:T(8,128)(2,1)}, bf16[256,128]{1,0:T(8,128)(2,1)S(1)}, u32[]{:S(2)}, u32[]{:S(2)}) collective-permute-start(bf16[256,128]{1,0:T(8,128)(2,1)} %param.16), channel_id=1, source_target_pairs={{0,16},{8,24},{16,32},{24,40},{32,48},{40,56},{48,64},{56,72},{64,... | collective-permute-start | bytes 196616 | tf_op jit(solution)/shard_map/ppermute | solution.py:18
  78.4 37.2 %collective-permute-start.2 = (bf16[256,128]{1,0:T(8,128)(2,1)}, bf16[256,128]{1,0:T(8,128)(2,1)}, u32[]{:S(2)}, u32[]{:S(2)}) collective-permute-start(bf16[256,128]{1,0:T(8,128)(2,1)} %param.16), channel_id=1, source_target_pairs={{0,24},{8,32},{16,40},{24,48},{32,56},{40,64},{48,72},{56,80},{64,... | collective-permute-start | bytes 196616 | tf_op jit(solution)/shard_map/ppermute | solution.py:18
  107.2 23.8 %all-to-all-start.1 = ((bf16[640,8,128]{0,2,1:T(8,128)(2,1)}), bf16[640,8,128]{0,2,1:T(8,128)(2,1)}, u32[]{:S(2)}, u32[]{:S(2)}) async-start(bf16[640,8,128]{0,2,1:T(8,128)(2,1)} %bitcast.861), calls=%async_computation.1 | async-start | bytes 2621440 | tf_op jit(solution)/shard_map/all_to_all | solution.py:105
  113.1 259.5 %reduce-scatter.3.cloned.1.call-start = ((), (), s32[]{:S(2)}) async-start(), calls=%async_computation.8 | async-start | bytes 2785280 | tf_op jit(solution)/shard_map/reduce_scatter | solution.py:196
  115.6 6.1 %collective-permute-start.3 = (bf16[256,128]{1,0:T(8,128)(2,1)}, bf16[256,128]{1,0:T(8,128)(2,1)S(1)}, u32[]{:S(2)}, u32[]{:S(2)}) collective-permute-start(bf16[256,128]{1,0:T(8,128)(2,1)} %param.16), channel_id=1, source_target_pairs={{0,32},{8,40},{16,48},{24,56},{32,64},{40,72},{48,80},{56,88},{64,... | collective-permute-start | bytes 196616 | tf_op jit(solution)/shard_map/ppermute | solution.py:18
  285.5 163.2 %reduce-scatter.5.cloned.1.call-start = ((), (), s32[]{:S(2)}) async-start(), calls=%async_computation.9 | async-start | bytes 2785280 | tf_op jit(solution)/shard_map/reduce_scatter | solution.py:199
  295.1 26.9 %collective-permute-start.12 = (f32[256,128]{1,0:T(8,128)}, f32[256,128]{1,0:T(8,128)}, u32[]{:S(2)}, u32[]{:S(2)}) collective-permute-start(f32[256,128]{1,0:T(8,128)} %convolution_bitcast_fusion.13), channel_id=1, source_target_pairs={{8,0},{16,8},{24,16},{32,24},{40,32},{48,40},{56,48},{64,56},{72,6... | collective-permute-start | bytes 393224 | tf_op jit(solution)/shard_map/ppermute | solution.py:18
  296.4 26.9 %collective-permute-start.13 = (f32[256,128]{1,0:T(8,128)}, f32[256,128]{1,0:T(8,128)}, u32[]{:S(2)}, u32[]{:S(2)}) collective-permute-start(f32[256,128]{1,0:T(8,128)} %convolution_bitcast_fusion.12), channel_id=1, source_target_pairs={{16,0},{24,8},{32,16},{40,24},{48,32},{56,40},{64,48},{72,56},{80,... | collective-permute-start | bytes 393224 | tf_op jit(solution)/shard_map/ppermute | solution.py:18
  297.7 27.0 %collective-permute-start.14 = (f32[256,128]{1,0:T(8,128)}, f32[256,128]{1,0:T(8,128)}, u32[]{:S(2)}, u32[]{:S(2)}) collective-permute-start(f32[256,128]{1,0:T(8,128)} %convolution_bitcast_fusion.11), channel_id=1, source_target_pairs={{24,0},{32,8},{40,16},{48,24},{56,32},{64,40},{72,48},{80,56},{88,... | collective-permute-start | bytes 393224 | tf_op jit(solution)/shard_map/ppermute | solution.py:18
  299.0 27.0 %collective-permute-start.15 = (f32[256,128]{1,0:T(8,128)}, f32[256,128]{1,0:T(8,128)}, u32[]{:S(2)}, u32[]{:S(2)}) collective-permute-start(f32[256,128]{1,0:T(8,128)} %convolution_bitcast_fusion.10), channel_id=1, source_target_pairs={{32,0},{40,8},{48,16},{56,24},{64,32},{72,40},{80,48},{88,56},{96,... | collective-permute-start | bytes 393224 | tf_op jit(solution)/shard_map/ppermute | solution.py:18
  304.0 76.0 %collective-permute-start.8 = (f32[256,128]{1,0:T(8,128)}, f32[256,128]{1,0:T(8,128)}, u32[]{:S(2)}, u32[]{:S(2)}) collective-permute-start(f32[256,128]{1,0:T(8,128)} %convolution_bitcast_fusion.18), channel_id=1, source_target_pairs={{8,0},{16,8},{24,16},{32,24},{40,32},{48,40},{56,48},{64,56},{72,6... | collective-permute-start | bytes 393224 | tf_op jit(solution)/shard_map/ppermute | solution.py:18
  322.0 58.0 %collective-permute-start.9 = (f32[256,128]{1,0:T(8,128)}, f32[256,128]{1,0:T(8,128)S(1)}, u32[]{:S(2)}, u32[]{:S(2)}) collective-permute-start(f32[256,128]{1,0:T(8,128)} %convolution_bitcast_fusion.17), channel_id=1, source_target_pairs={{16,0},{24,8},{32,16},{40,24},{48,32},{56,40},{64,48},{72,56},{80,... | collective-permute-start | bytes 393224 | tf_op jit(solution)/shard_map/ppermute | solution.py:18
  323.3 56.7 %collective-permute-start.10 = (f32[256,128]{1,0:T(8,128)}, f32[256,128]{1,0:T(8,128)S(1)}, u32[]{:S(2)}, u32[]{:S(2)}) collective-permute-start(f32[256,128]{1,0:T(8,128)} %convolution_bitcast_fusion.16), channel_id=1, source_target_pairs={{24,0},{32,8},{40,16},{48,24},{56,32},{64,40},{72,48},{80,56},{88,... | collective-permute-start | bytes 393224 | tf_op jit(solution)/shard_map/ppermute | solution.py:18
  324.6 55.4 %collective-permute-start.11 = (f32[256,128]{1,0:T(8,128)}, f32[256,128]{1,0:T(8,128)S(1)}, u32[]{:S(2)}, u32[]{:S(2)}) collective-permute-start(f32[256,128]{1,0:T(8,128)} %convolution_bitcast_fusion.15), channel_id=1, source_target_pairs={{32,0},{40,8},{48,16},{56,24},{64,32},{72,40},{80,48},{88,56},{96,... | collective-permute-start | bytes 393224 | tf_op jit(solution)/shard_map/ppermute | solution.py:18
  374.1 76.1 %all-to-all-start.2 = ((bf16[8,40,128]{2,1,0:T(8,128)(2,1)}), bf16[8,40,128]{2,1,0:T(8,128)(2,1)S(1)}, u32[]{:S(2)}, u32[]{:S(2)}) async-start(bf16[8,40,128]{2,1,0:T(8,128)(2,1)} %bitcast.123), calls=%async_computation.3 | async-start | bytes 163840 | tf_op jit(solution)/shard_map/all_to_all | solution.py:204
  450.3 11.1 %all-to-all-start.3 = ((bf16[8,40,128]{2,1,0:T(8,128)(2,1)}), bf16[8,40,128]{2,1,0:T(8,128)(2,1)S(1)}, u32[]{:S(2)}, u32[]{:S(2)}) async-start(bf16[8,40,128]{2,1,0:T(8,128)(2,1)} %bitcast.126), calls=%async_computation.5 | async-start | bytes 163840 | tf_op jit(solution)/shard_map/all_to_all | solution.py:207
  (31 other events, 136.4 us)
Sparse Core Ops, SparseCore 0:
  10.5 47.2 all-gather.2
  60.2 44.4 all-gather.4
  285.6 86.9 reduce-scatter.2
  376.4 72.2 reduce-scatter.4
where the time goes:
time: 472 us; the launch traced here: 469 us
  matrix products  171 us (36%)
  waiting for transfers between devices  169 us (36%)
  starting transfers between devices  59.8 us (13%)
  local copies, waits for them, and re-layouts  35.1 us (7%)
  other arithmetic  18.5 us (4%)
  between operations  14.4 us (3%)
    reduce_scatter x1, waiting for transfers between devices, shards(): lax.psum_scatter(value_grads.reshape(prompt_len, kv_cols), 'seq', scatter...  66.4 us
    reduce_scatter x1, waiting for transfers between devices, shards(): lax.psum_scatter(key_grads.reshape(prompt_len, kv_cols), 'seq', scatter_d...  44.4 us
    dot_general x15, matrix products, block_output(): jnp.einsum('qngk,knd->qngd', weights.astype(jnp.bfloat16), values, prefer...  39.7 us
    dot_general x25, matrix products, masked_scores(): jnp.einsum('qngd,knd->qngk', queries, key_rows, preferred_element_type=jn...  38.7 us
    ppermute x16, starting transfers between devices, passed_along(): return lax.ppermute(array, axis, pairs)  35.9 us
    all_gather x1, waiting for transfers between devices, shards(): lax.all_gather(prompt_v, 'seq', axis=0, tiled=True)  29 us
    dot_general x15, matrix products, grad_kv_of(): jnp.einsum('qngk,qngd->knd', rounded, cotangent, preferred_element_type=j...  25 us
    dot_general x15, matrix products, block_backward(): jnp.einsum('qngd,knd->qngk', cotangent, values, preferred_element_type=jn...  24.3 us
  transfers between devices with their start and end apart: 24, of which 6 were waited for; matrix products, arithmetic and copies ran while one was open for 28% of the time, Pallas kernels for 0%

commit v1 on v0

v1 whole, which is shorter than its diff:
```python
import functools
import math

import jax
import jax.numpy as jnp
from jax import lax
from jax.experimental import pallas as pl
from jax.experimental.pallas import tpu as pltpu
from jax.sharding import PartitionSpec as P

HD = 128
GROUP = 8
HEADS = 8
ROWS = 256
SPAN = 4
BLOCK = 320
SLAB = 40
CHUNK = 1280
CHUNKS = 5
KEYS = CHUNK * CHUNKS
SCALE = 1.0 / math.sqrt(HD)
EXP2_SCALE = SCALE * math.log2(math.e)
MASKED = -1e30
MESH = pl.DeviceIdType.MESH
F32 = jnp.float32
BF16 = jnp.bfloat16

CHIPS = {1: ((0, 0), (0, 1)), 2: ((0, 3), (0, 2)), 3: ((1, 0), (1, 1)), 4: ((1, 3), (1, 2))}
PLACE = {
    chip: chunk * CHUNK + i * 2 * BLOCK for chunk, two in CHIPS.items() for i, chip in enumerate(two)
}


def dot(a, b):
    return lax.dot_general(a, b, (((1,), (0,)), ((), ())), preferred_element_type=F32)


def key_rows(chunk):
    return pl.ds(pl.multiple_of(chunk * CHUNK, CHUNK), CHUNK)


def kernel(
    lengths,
    prompt_k,
    prompt_v,
    q_hbm,
    resp_k_hbm,
    resp_v_hbm,
    cot_hbm,
    out_ref,
    grad_q_ref,
    grad_k_resp,
    grad_v_resp,
    grad_k_prompt,
    grad_v_prompt,
    q_in,
    cot_in,
    kv,
    k_cols,
    v_cols,
    q_cols,
    q_rows,
    cot_cols,
    cot_scaled,
    cot_rows,
    weights,
    wide_a,
    wide_b,
    mask,
    run_max,
    chunk_max,
    acc,
    delta,
    slab_out,
    slab_in,
    partial,
    from_core,
    from_y,
    from_x,
    to_x,
    from_resp,
    back_out,
    back_in,
    local_sem,
    send_sem,
    recv_sem,
):
    seq = lax.axis_index("seq")
    head = lax.axis_index("head")
    core = seq % 2
    y = (seq // 2) % 4
    x = seq // 8
    first_row = seq * ROWS

    def at(dx, dy, dc):
        return ((((x + dx) % 2) * 4 + (y + dy) % 4) * 2 + (core + dc) % 2, head)

    names = {}

    def link(name, src, dst, device):
        index = names.setdefault(name, len(names))
        return pltpu.make_async_remote_copy(
            src_ref=src,
            dst_ref=dst,
            send_sem=send_sem.at[index],
            recv_sem=recv_sem.at[index],
            device_id=device,
            device_id_type=MESH,
        )

    def slab_link(i):
        return link(("slab", i), slab_out.at[i], slab_in.at[i], (seq, (head + i) % HEADS))

    def resp_link(d):
        return link(
            ("resp", d),
            kv.at[:, pl.ds(SPAN * ROWS, ROWS), :],
            kv.at[:, pl.ds((SPAN - d) * ROWS, ROWS), :],
            ((seq + d) % 16, head),
        )

    def block(chip, dc):
        return kv.at[:, pl.ds(PLACE[chip] + dc * BLOCK, BLOCK), :]

    def y_link(dx, dy):
        return link(("y", dx, dy), block((dx, 0), 0), block((dx, dy), 0), at(0, -dy, 0))

    def x_link():
        return link(("x",), block((0, 0), 0), block((1, 0), 0), at(1, 0, 0))

    def core_link(chip):
        return link(("core", chip), block(chip, 0), block(chip, 1), at(0, 0, 1))

    def core_back(chip):
        row = PLACE[chip] - CHUNK
        return link(
            ("core_back", chip),
            partial.at[:, pl.ds(PLACE[chip] + BLOCK, BLOCK), :],
            from_core.at[:, pl.ds(row // 2, BLOCK), :],
            at(0, 0, 1),
        )

    def y_back(dx, dy):
        return link(
            ("y_back", dx, dy),
            partial.at[:, pl.ds(PLACE[(dx, dy)], BLOCK), :],
            from_y.at[dx, dy - 1],
            at(0, dy, 0),
        )

    def x_back():
        return link(("x_back",), to_x, from_x, at(1, 0, 0))

    def resp_back(d):
        return link(
            ("resp_back", d),
            partial.at[:, pl.ds((SPAN - d) * ROWS, ROWS), :],
            from_resp.at[d - 1],
            ((seq + 16 - d) % 16, head),
        )

    def slab_back(i):
        return link(
            ("slab_back", i), back_out.at[i], back_in.at[i], (seq, (head + HEADS - i) % HEADS)
        )

    loads = [
        pltpu.make_async_copy(
            resp_k_hbm, kv.at[0, pl.ds(SPAN * ROWS, ROWS), :], local_sem.at[0]
        ),
        pltpu.make_async_copy(
            resp_v_hbm, kv.at[1, pl.ds(SPAN * ROWS, ROWS), :], local_sem.at[1]
        ),
        pltpu.make_async_copy(q_hbm, q_in, local_sem.at[2]),
        pltpu.make_async_copy(cot_hbm, cot_in, local_sem.at[3]),
    ]
    for load in loads:
        load.start()
    barrier = pltpu.get_barrier_semaphore()
    for i in range(1, 16):
        pl.semaphore_signal(
            barrier, inc=1, device_id=((seq + i) % 16, head), device_id_type=MESH
        )
    for i in range(1, HEADS):
        pl.semaphore_signal(
            barrier, inc=1, device_id=(seq, (head + i) % HEADS), device_id_type=MESH
        )
    for i in range(HEADS):
        columns = pl.ds(pl.multiple_of(((head + i) % HEADS) * HD, HD), HD)
        slab_out[i, 0] = prompt_k[:, columns].astype(F32)
        slab_out[i, 1] = prompt_v[:, columns].astype(F32)
    pl.semaphore_wait(barrier, 15 + HEADS - 1)
    for i in range(1, HEADS):
        slab_link(i).start()
    loads[0].wait()
    loads[1].wait()
    for d in range(1, SPAN + 1):
        resp_link(d).start()

    loads[2].wait()
    loads[3].wait()
    for g in range(GROUP):
        columns = slice(g * HD, (g + 1) * HD)
        q_rows[g * ROWS : (g + 1) * ROWS, :] = q_in[:, columns]
        q_cols[g] = q_in[:, columns].T
        cot_cols[g] = cot_in[:, columns].astype(F32).T
    token = first_row + lax.broadcasted_iota(jnp.int32, (1, ROWS), 1)
    start = jnp.zeros((1, ROWS), jnp.int32)
    end = jnp.int32(0)
    for i in range(8):
        end = end + lengths[i]
        start = jnp.where(token >= end, end, start)
    key = first_row - SPAN * ROWS + lax.broadcasted_iota(jnp.int32, (CHUNK, ROWS), 0)
    mask[...] = jnp.where((key >= start) & (key <= token), 0.0, MASKED)
    run_max[...] = jnp.full_like(run_max, MASKED)
    acc[...] = jnp.zeros_like(acc)
    cot_scaled[...] = jnp.zeros_like(cot_scaled)
    ones_row = lax.broadcasted_iota(jnp.int32, (16, KEYS), 0) == 0
    v_cols[HD:, :] = jnp.where(ones_row, 1.0, 0.0).astype(BF16)

    for i in range(1, HEADS):
        slab_link(i).wait_recv()
    own = PLACE[(0, 0)]
    for i in range(2):
        slabs = [slab_out[0, i]] + [slab_in[j, i] for j in range(1, HEADS)]
        kv[i, own : own + BLOCK, :] = jnp.concatenate(slabs, axis=0).astype(BF16)
    core_link((0, 0)).start()
    for dy in (1, 3):
        y_link(0, dy).start()
    x_link().start()
    y_link(0, 2).start()

    def turn(chunk):
        rows = key_rows(chunk)
        k_cols[:, rows] = kv[0, rows, :].T
        v_cols[:HD, rows] = kv[1, rows, :].T

    def forward(chunk, masked):
        rows = key_rows(chunk)
        wide = (wide_a, wide_b)

        def scores(g):
            s = dot(kv[0, rows, :], q_cols[g])
            if masked:
                s = s + mask[...]
            wide[g % 2][...] = s
            earlier = run_max[g : g + 1, :]
            largest = jnp.maximum(earlier, jnp.max(s, axis=0, keepdims=True))
            run_max[g : g + 1, :] = largest
            chunk_max[chunk, g : g + 1, :] = largest
            return largest, jnp.exp2((earlier - largest) * EXP2_SCALE)

        def output(g, shrink):
            part = dot(v_cols[:, rows], weights[rows, g * ROWS : (g + 1) * ROWS])
            acc[g] = acc[g] * shrink + part

        largest, shrink = scores(0)
        last = None
        for g in range(GROUP):
            if g + 1 < GROUP:
                following = scores(g + 1)
            w = jnp.exp2((wide[g % 2][...] - largest) * EXP2_SCALE)
            weights[rows, g * ROWS : (g + 1) * ROWS] = w.astype(BF16)
            if last is not None:
                output(g - 1, last)
            last = shrink
            if g + 1 < GROUP:
                largest, shrink = following
        output(GROUP - 1, last)

    for d in range(1, SPAN + 1):
        resp_link(d).wait_recv()
    turn(0)
    forward(0, True)

    def prompt_chunk(chunk, carry):
        @pl.when(chunk == 1)
        def _():
            for dy in (1, 3):
                y_link(0, dy).wait_recv()
                core_link((0, dy)).start()
            core_link((0, 0)).wait_recv()
            core_link((0, 1)).wait_recv()

        @pl.when(chunk == 2)
        def _():
            x_link().wait_recv()
            for dy in (1, 3, 2):
                y_link(1, dy).start()
            core_link((1, 0)).start()
            y_link(0, 2).wait_recv()
            core_link((0, 2)).start()
            core_link((0, 3)).wait_recv()
            core_link((0, 2)).wait_recv()

        @pl.when(chunk == 3)
        def _():
            for dy in (1, 3):
                y_link(1, dy).wait_recv()
                core_link((1, dy)).start()
            core_link((1, 0)).wait_recv()
            core_link((1, 1)).wait_recv()

        @pl.when(chunk == 4)
        def _():
            y_link(1, 2).wait_recv()
            core_link((1, 2)).start()
            core_link((1, 3)).wait_recv()
            core_link((1, 2)).wait_recv()

        turn(chunk)
        forward(chunk, False)
        return carry

    lax.fori_loop(1, CHUNKS, prompt_chunk, 0)

    for g in range(GROUP):
        inverse = 1.0 / acc[g, HD : HD + 1, :]
        rounded = (acc[g, :HD, :] * inverse).astype(BF16)
        out_ref[:, g * HD : (g + 1) * HD] = rounded.T
        delta[g : g + 1, :] = jnp.sum(cot_cols[g] * rounded.astype(F32), axis=0, keepdims=True)
        for chunk in range(CHUNKS):
            chunk_max[chunk, g : g + 1, :] = inverse * jnp.exp2(
                (chunk_max[chunk, g : g + 1, :] - run_max[g : g + 1, :]) * EXP2_SCALE
            )

    is_one = lax.broadcasted_iota(jnp.int32, (CHUNK, HD), 1) < 3
    ones_columns = jnp.where(is_one, 1.0, 0.0).astype(BF16)

    def pair_sum(chip):
        core_back(chip).wait_recv()
        row = PLACE[chip]
        half = (row - CHUNK) // 2
        mine = partial[:, row : row + BLOCK, :].astype(F32)
        partial[:, row : row + BLOCK, :] = (
            mine + from_core[:, half : half + BLOCK, :].astype(F32)
        ).astype(BF16)

    def backward(step, carry):
        chunk = CHUNKS - 1 - step
        rows = key_rows(chunk)
        for g in range(GROUP):
            factor = chunk_max[chunk, g : g + 1, :]
            scaled = (cot_cols[g] * factor).astype(BF16)
            cot_scaled[g, :HD, :] = scaled
            cot_rows[g * ROWS : (g + 1) * ROWS, :] = scaled.T
            rest = -(factor * delta[g : g + 1, :])
            for i in range(3):
                piece = rest.astype(BF16)
                cot_scaled[g, HD + i : HD + i + 1, :] = piece
                rest = rest - piece.astype(F32)
        partial[1, rows, :] = dot(weights[rows, :], cot_rows[...]).astype(BF16)
        values = jnp.concatenate([kv[1, rows, :], ones_columns], axis=1)
        wide = (wide_a, wide_b)
        wide[0][...] = dot(values, cot_scaled[0])
        for g in range(GROUP):
            if g + 1 < GROUP:
                wide[(g + 1) % 2][...] = dot(values, cot_scaled[g + 1])
            columns = slice(g * ROWS, (g + 1) * ROWS)
            weights[rows, columns] = (
                weights[rows, columns].astype(F32) * wide[g % 2][...]
            ).astype(BF16)

        for earlier in (4, 3, 2, 1):

            @pl.when(chunk == earlier - 1)
            def _():
                for chip in CHIPS[earlier]:
                    pair_sum(chip)
                    if chip[1] != 0:
                        y_back(*chip).start()

        partial[0, rows, :] = (dot(weights[rows, :], q_rows[...]) * SCALE).astype(BF16)

        for done in (4, 3, 2, 1):

            @pl.when(chunk == done)
            def _():
                for chip in CHIPS[done]:
                    core_back(chip).start()

        return carry

    lax.fori_loop(0, CHUNKS, backward, 0)

    for d in range(SPAN, 0, -1):
        resp_back(d).start()
    place = PLACE[(1, 0)]
    total = partial[:, place : place + BLOCK, :].astype(F32)
    for dy in (1, 2, 3):
        y_back(1, dy).wait_recv()
        total = total + from_y[1, dy - 1].astype(F32)
    to_x[...] = total.astype(BF16)
    x_back().start()

    def grad_query(g):
        turned = dot(k_cols[...], weights[:, g * ROWS : (g + 1) * ROWS]) * SCALE
        grad_q_ref[:, g * HD : (g + 1) * HD] = turned.astype(BF16).T

    for g in range(GROUP):
        grad_query(g)

    total = partial[:, own : own + BLOCK, :].astype(F32)
    for dy in (1, 2, 3):
        y_back(0, dy).wait_recv()
        total = total + from_y[0, dy - 1].astype(F32)
    x_back().wait_recv()
    total = total + from_x[...].astype(F32)
    for i in range(HEADS):
        back_out[i] = total[:, i * SLAB : (i + 1) * SLAB, :]
    for i in range(1, HEADS):
        slab_back(i).start()

    total = partial[:, SPAN * ROWS : CHUNK, :].astype(F32)
    for d in range(1, SPAN + 1):
        resp_back(d).wait_recv()
        total = total + from_resp[d - 1].astype(F32)
    grad_k_resp[...] = total[0].astype(BF16)
    grad_v_resp[...] = total[1].astype(BF16)

    for i in range(HEADS):
        if i > 0:
            slab_back(i).wait_recv()
        source = back_out if i == 0 else back_in
        columns = pl.ds(pl.multiple_of(((head + i) % HEADS) * HD, HD), HD)
        grad_k_prompt[:, columns] = source[i, 0].astype(BF16)
        grad_v_prompt[:, columns] = source[i, 1].astype(BF16)

    for i in range(1, HEADS):
        slab_link(i).wait_send()
        slab_back(i).wait_send()
    for d in range(1, SPAN + 1):
        resp_link(d).wait_send()
        resp_back(d).wait_send()
    for chip in PLACE:
        core_link(chip).wait_send()
        core_back(chip).wait_send()
        if chip[1] != 0:
            y_link(*chip).wait_send()
            y_back(*chip).wait_send()
    x_link().wait_send()
    x_back().wait_send()


def shards(prompt_k, prompt_v, resp_q, resp_k, resp_v, grad_out, resp_lengths):
    vmem = pl.BlockSpec(memory_space=pltpu.VMEM)
    anywhere = pl.BlockSpec(memory_space=pl.ANY)
    links = 2 * (HEADS - 1) + 2 * SPAN + 2 * (6 + 1 + 8)
    like = jax.ShapeDtypeStruct
    return pl.pallas_call(
        kernel,
        out_shape=(
            like((ROWS, GROUP * HD), BF16),
            like((ROWS, GROUP * HD), BF16),
            like((ROWS, HD), BF16),
            like((ROWS, HD), BF16),
            like((SLAB, HEADS * HD), BF16),
            like((SLAB, HEADS * HD), BF16),
        ),
        in_specs=[pl.BlockSpec(memory_space=pltpu.SMEM), vmem, vmem] + [anywhere] * 4,
        out_specs=[vmem] * 6,
        scratch_shapes=[
            pltpu.VMEM((ROWS, GROUP * HD), BF16),
            pltpu.VMEM((ROWS, GROUP * HD), BF16),
            pltpu.VMEM((2, KEYS, HD), BF16),
            pltpu.VMEM((HD, KEYS), BF16),
            pltpu.VMEM((HD + 16, KEYS), BF16),
            pltpu.VMEM((GROUP, HD, ROWS), BF16),
            pltpu.VMEM((GROUP * ROWS, HD), BF16),
            pltpu.VMEM((GROUP, HD, ROWS), F32),
            pltpu.VMEM((GROUP, 2 * HD, ROWS), BF16),
            pltpu.VMEM((GROUP * ROWS, HD), BF16),
            pltpu.VMEM((KEYS, GROUP * ROWS), BF16),
            pltpu.VMEM((CHUNK, ROWS), F32),
            pltpu.VMEM((CHUNK, ROWS), F32),
            pltpu.VMEM((CHUNK, ROWS), F32),
            pltpu.VMEM((GROUP, ROWS), F32),
            pltpu.VMEM((CHUNKS, GROUP, ROWS), F32),
            pltpu.VMEM((GROUP, HD + 16, ROWS), F32),
            pltpu.VMEM((GROUP, ROWS), F32),
            pltpu.VMEM((HEADS, 2, SLAB, HD), F32),
            pltpu.VMEM((HEADS, 2, SLAB, HD), F32),
            pltpu.VMEM((2, KEYS, HD), BF16),
            pltpu.VMEM((2, 8 * BLOCK, HD), BF16),
            pltpu.VMEM((2, 3, 2, BLOCK, HD), BF16),
            pltpu.VMEM((2, BLOCK, HD), BF16),
            pltpu.VMEM((2, BLOCK, HD), BF16),
            pltpu.VMEM((SPAN, 2, ROWS, HD), BF16),
            pltpu.VMEM((HEADS, 2, SLAB, HD), F32),
            pltpu.VMEM((HEADS, 2, SLAB, HD), F32),
            pltpu.SemaphoreType.DMA((4,)),
            pltpu.SemaphoreType.DMA((links,)),
            pltpu.SemaphoreType.DMA((links,)),
        ],
        compiler_params=pltpu.CompilerParams(
            collective_id=0, has_side_effects=True, vmem_limit_bytes=60 * 2**20
        ),
        cost_estimate=pl.CostEstimate(
            flops=12 * ROWS * GROUP * KEYS * HD,
            bytes_accessed=4 * 2**20,
            transcendentals=ROWS * GROUP * KEYS,
        ),
        name="shared_prompt_attention",
    )(resp_lengths, prompt_k, prompt_v, resp_q, resp_k, resp_v, grad_out)


def solution(mesh):
    placed = (
        P(("seq", "head"), None),
        P(("seq", "head"), None),
        P("seq", "head"),
        P("seq", "head"),
        P("seq", "head"),
        P("seq", "head"),
        P(),
    )
    return jax.shard_map(
        shards,
        mesh=mesh,
        in_specs=placed,
        out_specs=(
            P("seq", "head"),
            P("seq", "head"),
            P("seq", "head"),
            P("seq", "head"),
            P(("seq", "head"), None),
            P(("seq", "head"), None),
        ),
        check_vma=False,
    )
```

time: 472 us -> 129 us (0.27)
  matrix products: 171 us -> 0 us
  waiting for transfers between devices: 169 us -> 0 us
  Pallas kernels: 0 us -> 122 us
  starting transfers between devices: 59.8 us -> 0 us
  local copies, waits for them, and re-layouts: 35.1 us -> 6.11 us
  other arithmetic: 18.5 us -> 0 us
  between operations: 14.4 us -> 0.66 us
    dot_general x100 -> x0, matrix products: 171 us -> none  [the longest x15 39.7 us: block_output(): jnp.einsum('qngk,knd->qngd', weights.astype(jnp.bfloat16), values, prefer...]
    pallas_call x0 -> x1, Pallas kernels: none -> 122 us  [shards(): pl.pallas_call(kernel, out_shape=(like((ROWS, GROUP * HD), BF16), like((R...]
    reduce_scatter x2 -> x0, waiting for transfers between devices: 111 us -> none  [the longest x1 66.4 us: shards(): lax.psum_scatter(value_grads.reshape(prompt_len, kv_cols), 'seq', scatter...]
    all_gather x2 -> x0, waiting for transfers between devices: 50.8 us -> none  [the longest x1 29 us: shards(): lax.all_gather(prompt_v, 'seq', axis=0, tiled=True)]
    ppermute x16 -> x0, starting transfers between devices: 35.9 us -> none  [passed_along(): return lax.ppermute(array, axis, pairs)]
    all_to_all x4 -> x0, starting transfers between devices: 23.6 us -> none  [the longest x1 5.9 us: shards(): lax.all_to_all(summed_v.astype(jnp.bfloat16), 'head', split_axis=0, conca...]
    unnamed x69 -> x16, local copies, waits for them, and re-layouts: 19 us -> 6.11 us
    reduce_sum x16 -> x0, other arithmetic: 12.2 us -> none  [the longest x15 12.1 us: block_stats(): row_total = jnp.sum(jnp.exp(scores - row_max[..., None]), axis=-1)]
  transfers between devices with their start and end apart: 24 -> 0, of which waited for: 6 -> 0; matrix products, arithmetic and copies ran while one was open for 28% -> 0% of each run, Pallas kernels for 0% -> 0%
where the time goes in v1:
time: 129 us; the launch traced here: 128 us
  Pallas kernels  122 us (95%)
  local copies, waits for them, and re-layouts  6.11 us (5%)
    pallas_call x1, Pallas kernels, shards(): pl.pallas_call(kernel, out_shape=(like((ROWS, GROUP * HD), BF16), like((R...  122 us
    unnamed x16, local copies, waits for them, and re-layouts  6.11 us

profile of v1, /device:TPU:2, one launch (start us, length us, event | category | flops | bytes accessed | tf_op | source)
XLA Modules:
  0.0 128.3 jit_solution(8686436232077990350)
XLA Ops:
  0.6 121.5 %shared_prompt_attention.1 = (bf16[256,1024]{1,0:T(8,128)(2,1)}, bf16[256,1024]{1,0:T(8,128)(2,1)}, bf16[256,128]{1,0:T(8,128)(2,1)}, bf16[256,128]{1,0:T(8,128)...) custom-call(s32[8]{0:T(128)} %lengths.1, bf16[40,1024]{1,0:T(8,128)(2,1)} %prompt_k.1, ...), custom_call_target="tpu_custom_call" | custom-call | flops 20132659200 | bytes 4194304 | tf_op jit(solution)/shard_map/shared_prompt_attention/pallas_call | solution.py:450
  122.2 0.0 copy-start
  122.2 1.9 %copy.19 = bf16[256,1024]{1,0:T(8,128)(2,1)} copy(bf16[256,1024]{1,0:T(8,128)(2,1)} %get-tuple-element.12) | data formatting | bytes 1048576
  124.1 0.0 copy-done
  124.1 0.0 copy-start.4
  124.1 0.8 copy.20
  124.9 0.1 copy-done.4
  125.0 0.0 copy-start.3
  125.0 0.6 copy.21
  125.6 0.2 copy-done.3
  125.8 0.0 copy-start.2
  125.8 0.6 copy.22
  126.5 0.3 copy-done.2
  126.8 0.0 copy-start.1
  126.8 0.6 copy.23
  127.4 0.3 copy-done.1
  127.7 0.6 copy.24
Async XLA Ops:
  122.2 1.9 %copy-start = (bf16[256,1024]{1,0:T(8,128)(2,1)S(1)}, bf16[256,1024]{1,0:T(8,128)(2,1)}, u32[]{:S(2)}) copy-start(bf16[256,1024]{1,0:T(8,128)(2,1)} %get-tuple-element.13) | copy-start | bytes 1572868
  124.1 0.9 copy-start.4
  125.0 0.9 copy-start.3
  125.8 0.9 copy-start.2
  126.8 0.9 copy-start.1

commit v2 on v1

--- a/solution.py
+++ b/solution.py
@@ -61,16 +61,15 @@
     q_cols,
     q_rows,
     cot_cols,
-    cot_scaled,
     cot_rows,
     weights,
+    scaled,
     wide_a,
     wide_b,
     mask,
     run_max,
     chunk_max,
     acc,
-    delta,
     slab_out,
     slab_in,
     partial,
@@ -79,6 +78,7 @@
     from_x,
     to_x,
     from_resp,
+    from_core_resp,
     back_out,
     back_in,
     local_sem,
@@ -111,13 +111,17 @@
     def slab_link(i):
         return link(("slab", i), slab_out.at[i], slab_in.at[i], (seq, (head + i) % HEADS))
 
+    def resp_rows(ref, d):
+        return ref.at[:, pl.ds(pl.multiple_of((SPAN - d) * ROWS, ROWS), ROWS), :]
+
     def resp_link(d):
         return link(
-            ("resp", d),
-            kv.at[:, pl.ds(SPAN * ROWS, ROWS), :],
-            kv.at[:, pl.ds((SPAN - d) * ROWS, ROWS), :],
-            ((seq + d) % 16, head),
-        )
+            ("resp", d), resp_rows(kv, 0), resp_rows(kv, d), ((seq + d) % 16, head)
+        )
+
+    def core_resp_link(d):
+        source = 2 * core + d - 1
+        return link(("core_resp", d), resp_rows(kv, source), resp_rows(kv, d), at(0, 0, 1))
 
     def block(chip, dc):
         return kv.at[:, pl.ds(PLACE[chip] + dc * BLOCK, BLOCK), :]
@@ -151,11 +155,16 @@
     def x_back():
         return link(("x_back",), to_x, from_x, at(1, 0, 0))
 
+    def core_resp_back(d):
+        return link(
+            ("core_resp_back", d), resp_rows(partial, d), from_core_resp.at[d // 2], at(0, 0, 1)
+        )
+
     def resp_back(d):
         return link(
             ("resp_back", d),
-            partial.at[:, pl.ds((SPAN - d) * ROWS, ROWS), :],
-            from_resp.at[d - 1],
+            resp_rows(partial, d),
+            from_resp.at[d // 2 - 1],
             ((seq + 16 - d) % 16, head),
         )
 
@@ -177,24 +186,21 @@
     for load in loads:
         load.start()
     barrier = pltpu.get_barrier_semaphore()
-    for i in range(1, 16):
-        pl.semaphore_signal(
-            barrier, inc=1, device_id=((seq + i) % 16, head), device_id_type=MESH
-        )
-    for i in range(1, HEADS):
-        pl.semaphore_signal(
-            barrier, inc=1, device_id=(seq, (head + i) % HEADS), device_id_type=MESH
-        )
+    partners = [at(0, 0, 1), at(0, 1, 0), at(0, 2, 0), at(0, 3, 0), at(1, 0, 0)]
+    partners += [((seq + d) % 16, head) for d in (2, 4, 12, 14)]
+    partners += [(seq, (head + i) % HEADS) for i in range(1, HEADS)]
+    for partner in partners:
+        pl.semaphore_signal(barrier, inc=1, device_id=partner, device_id_type=MESH)
     for i in range(HEADS):
         columns = pl.ds(pl.multiple_of(((head + i) % HEADS) * HD, HD), HD)
-        slab_out[i, 0] = prompt_k[:, columns].astype(F32)
-        slab_out[i, 1] = prompt_v[:, columns].astype(F32)
-    pl.semaphore_wait(barrier, 15 + HEADS - 1)
+        two = (prompt_k[:, columns].astype(F32), prompt_v[:, columns].astype(F32))
+        slab_out[i] = jnp.concatenate(two, axis=0).astype(BF16)
+    pl.semaphore_wait(barrier, len(partners))
     for i in range(1, HEADS):
         slab_link(i).start()
     loads[0].wait()
     loads[1].wait()
-    for d in range(1, SPAN + 1):
+    for d in (4, 2):
         resp_link(d).start()
 
     loads[2].wait()
@@ -203,7 +209,9 @@
         columns = slice(g * HD, (g + 1) * HD)
         q_rows[g * ROWS : (g + 1) * ROWS, :] = q_in[:, columns]
         q_cols[g] = q_in[:, columns].T
-        cot_cols[g] = cot_in[:, columns].astype(F32).T
+        cot_rows[g * ROWS : (g + 1) * ROWS, :] = cot_in[:, columns]
+        cot_cols[g, :HD, :] = cot_in[:, columns].T
+        cot_cols[g, HD:, :] = jnp.zeros((HD, ROWS), BF16)
     token = first_row + lax.broadcasted_iota(jnp.int32, (1, ROWS), 1)
     start = jnp.zeros((1, ROWS), jnp.int32)
     end = jnp.int32(0)
@@ -214,16 +222,16 @@
     mask[...] = jnp.where((key >= start) & (key <= token), 0.0, MASKED)
     run_max[...] = jnp.full_like(run_max, MASKED)
     acc[...] = jnp.zeros_like(acc)
-    cot_scaled[...] = jnp.zeros_like(cot_scaled)
     ones_row = lax.broadcasted_iota(jnp.int32, (16, KEYS), 0) == 0
     v_cols[HD:, :] = jnp.where(ones_row, 1.0, 0.0).astype(BF16)
 
     for i in range(1, HEADS):
         slab_link(i).wait_recv()
     own = PLACE[(0, 0)]
+    slabs = [slab_out[0].astype(F32)] + [slab_in[i].astype(F32) for i in range(1, HEADS)]
     for i in range(2):
-        slabs = [slab_out[0, i]] + [slab_in[j, i] for j in range(1, HEADS)]
-        kv[i, own : own + BLOCK, :] = jnp.concatenate(slabs, axis=0).astype(BF16)
+        pieces = [slab[i * SLAB : (i + 1) * SLAB, :] for slab in slabs]
+        kv[i, own : own + BLOCK, :] = jnp.concatenate(pieces, axis=0).astype(BF16)
     core_link((0, 0)).start()
     for dy in (1, 3):
         y_link(0, dy).start()
@@ -232,10 +240,9 @@
 
     def turn(chunk):
         rows = key_rows(chunk)
-        k_cols[:, rows] = kv[0, rows, :].T
         v_cols[:HD, rows] = kv[1, rows, :].T
 
-    def forward(chunk, masked):
+    def forward(chunk, masked, middle=None):
         rows = key_rows(chunk)
         wide = (wide_a, wide_b)
 
@@ -264,47 +271,56 @@
             if last is not None:
                 output(g - 1, last)
             last = shrink
+            if middle is not None and g == GROUP // 2:
+                middle()
             if g + 1 < GROUP:
                 largest, shrink = following
         output(GROUP - 1, last)
 
-    for d in range(1, SPAN + 1):
+    for d in (2, 4):
         resp_link(d).wait_recv()
+    for d in (1, 3):
+        core_resp_link(d).start()
+
+    def pass_on():
+        x_link().wait_recv()
+        for dy in (1, 3, 2):
+            y_link(1, dy).start()
+        core_link((1, 0)).start()
+        for dy in (1, 3):
+            y_link(0, dy).wait_recv()
+            core_link((0, dy)).start()
+
+    for d in (1, 3):
+        core_resp_link(d).wait_recv()
     turn(0)
-    forward(0, True)
+    forward(0, True, pass_on)
 
     def prompt_chunk(chunk, carry):
         @pl.when(chunk == 1)
         def _():
-            for dy in (1, 3):
-                y_link(0, dy).wait_recv()
-                core_link((0, dy)).start()
+            y_link(0, 2).wait_recv()
+            core_link((0, 2)).start()
             core_link((0, 0)).wait_recv()
             core_link((0, 1)).wait_recv()
 
         @pl.when(chunk == 2)
-        def _():
-            x_link().wait_recv()
-            for dy in (1, 3, 2):
-                y_link(1, dy).start()
-            core_link((1, 0)).start()
-            y_link(0, 2).wait_recv()
-            core_link((0, 2)).start()
-            core_link((0, 3)).wait_recv()
-            core_link((0, 2)).wait_recv()
-
-        @pl.when(chunk == 3)
         def _():
             for dy in (1, 3):
                 y_link(1, dy).wait_recv()
                 core_link((1, dy)).start()
-            core_link((1, 0)).wait_recv()
-            core_link((1, 1)).wait_recv()
-
-        @pl.when(chunk == 4)
+            core_link((0, 3)).wait_recv()
+            core_link((0, 2)).wait_recv()
+
+        @pl.when(chunk == 3)
         def _():
             y_link(1, 2).wait_recv()
             core_link((1, 2)).start()
+            core_link((1, 0)).wait_recv()
+            core_link((1, 1)).wait_recv()
+
+        @pl.when(chunk == 4)
+        def _():
             core_link((1, 3)).wait_recv()
             core_link((1, 2)).wait_recv()
 
@@ -318,7 +334,12 @@
         inverse = 1.0 / acc[g, HD : HD + 1, :]
         rounded = (acc[g, :HD, :] * inverse).astype(BF16)
         out_ref[:, g * HD : (g + 1) * HD] = rounded.T
-        delta[g : g + 1, :] = jnp.sum(cot_cols[g] * rounded.astype(F32), axis=0, keepdims=True)
+        products = cot_cols[g, :HD, :].astype(F32) * rounded.astype(F32)
+        rest = -jnp.sum(products, axis=0, keepdims=True)
+        for i in range(3):
+            piece = rest.astype(BF16)
+            cot_cols[g, HD + i : HD + i + 1, :] = piece
+            rest = rest - piece.astype(F32)
         for chunk in range(CHUNKS):
             chunk_max[chunk, g : g + 1, :] = inverse * jnp.exp2(
                 (chunk_max[chunk, g : g + 1, :] - run_max[g : g + 1, :]) * EXP2_SCALE
@@ -336,31 +357,29 @@
             mine + from_core[:, half : half + BLOCK, :].astype(F32)
         ).astype(BF16)
 
+    def sum_over_y():
+        place = PLACE[(1, 0)]
+        total = partial[:, place : place + BLOCK, :].astype(F32)
+        for dy in (1, 2, 3):
+            y_back(1, dy).wait_recv()
+            total = total + from_y[1, dy - 1].astype(F32)
+        to_x[...] = total.astype(BF16)
+        x_back().start()
+
     def backward(step, carry):
         chunk = CHUNKS - 1 - step
         rows = key_rows(chunk)
-        for g in range(GROUP):
-            factor = chunk_max[chunk, g : g + 1, :]
-            scaled = (cot_cols[g] * factor).astype(BF16)
-            cot_scaled[g, :HD, :] = scaled
-            cot_rows[g * ROWS : (g + 1) * ROWS, :] = scaled.T
-            rest = -(factor * delta[g : g + 1, :])
-            for i in range(3):
-                piece = rest.astype(BF16)
-                cot_scaled[g, HD + i : HD + i + 1, :] = piece
-                rest = rest - piece.astype(F32)
-        partial[1, rows, :] = dot(weights[rows, :], cot_rows[...]).astype(BF16)
+        k_cols[:, rows] = kv[0, rows, :].T
         values = jnp.concatenate([kv[1, rows, :], ones_columns], axis=1)
         wide = (wide_a, wide_b)
-        wide[0][...] = dot(values, cot_scaled[0])
+        wide[0][...] = dot(values, cot_cols[0])
         for g in range(GROUP):
             if g + 1 < GROUP:
-                wide[(g + 1) % 2][...] = dot(values, cot_scaled[g + 1])
+                wide[(g + 1) % 2][...] = dot(values, cot_cols[g + 1])
             columns = slice(g * ROWS, (g + 1) * ROWS)
-            weights[rows, columns] = (
-                weights[rows, columns].astype(F32) * wide[g % 2][...]
-            ).astype(BF16)
-
+            w = weights[rows, columns].astype(F32) * chunk_max[chunk, g : g + 1, :]
+            scaled[:, columns] = w.astype(BF16)
+            weights[rows, columns] = (w * wide[g % 2][...]).astype(BF16)
         for earlier in (4, 3, 2, 1):
 
             @pl.when(chunk == earlier - 1)
@@ -370,7 +389,12 @@
                     if chip[1] != 0:
                         y_back(*chip).start()
 
+        partial[1, rows, :] = dot(scaled[...], cot_rows[...]).astype(BF16)
         partial[0, rows, :] = (dot(weights[rows, :], q_rows[...]) * SCALE).astype(BF16)
+
+        @pl.when(chunk == 0)
+        def _():
+            sum_over_y()
 
         for done in (4, 3, 2, 1):
 
@@ -383,21 +407,25 @@
 
     lax.fori_loop(0, CHUNKS, backward, 0)
 
-    for d in range(SPAN, 0, -1):
-        resp_back(d).start()
-    place = PLACE[(1, 0)]
-    total = partial[:, place : place + BLOCK, :].astype(F32)
-    for dy in (1, 2, 3):
-        y_back(1, dy).wait_recv()
-        total = total + from_y[1, dy - 1].astype(F32)
-    to_x[...] = total.astype(BF16)
-    x_back().start()
+    for d in (1, 3):
+        core_resp_back(d).start()
 
     def grad_query(g):
         turned = dot(k_cols[...], weights[:, g * ROWS : (g + 1) * ROWS]) * SCALE
         grad_q_ref[:, g * HD : (g + 1) * HD] = turned.astype(BF16).T
 
-    for g in range(GROUP):
+    for g in range(2):
+        grad_query(g)
+
+    for d in (1, 3):
+        core_resp_back(d).wait_recv()
+        near = pl.ds(pl.multiple_of((SPAN - (2 * core + d - 1)) * ROWS, ROWS), ROWS)
+        total = partial[:, near, :].astype(F32) + from_core_resp[d // 2].astype(F32)
+        partial[:, near, :] = total.astype(BF16)
+    for d in (4, 2):
+        resp_back(d).start()
+
+    for g in range(2, 6):
         grad_query(g)
 
     total = partial[:, own : own + BLOCK, :].astype(F32)
@@ -407,14 +435,18 @@
     x_back().wait_recv()
     total = total + from_x[...].astype(F32)
     for i in range(HEADS):
-        back_out[i] = total[:, i * SLAB : (i + 1) * SLAB, :]
+        two = [total[j, i * SLAB : (i + 1) * SLAB, :] for j in range(2)]
+        back_out[i] = jnp.concatenate(two, axis=0).astype(BF16)
     for i in range(1, HEADS):
         slab_back(i).start()
 
+    for g in range(6, GROUP):
+        grad_query(g)
+
     total = partial[:, SPAN * ROWS : CHUNK, :].astype(F32)
-    for d in range(1, SPAN + 1):
+    for d in (2, 4):
         resp_back(d).wait_recv()
-        total = total + from_resp[d - 1].astype(F32)
+        total = total + from_resp[d // 2 - 1].astype(F32)
     grad_k_resp[...] = total[0].astype(BF16)
     grad_v_resp[...] = total[1].astype(BF16)
 
@@ -422,16 +454,20 @@
         if i > 0:
             slab_back(i).wait_recv()
         source = back_out if i == 0 else back_in
+        slab = source[i].astype(F32)
         columns = pl.ds(pl.multiple_of(((head + i) % HEADS) * HD, HD), HD)
-        grad_k_prompt[:, columns] = source[i, 0].astype(BF16)
-        grad_v_prompt[:, columns] = source[i, 1].astype(BF16)
+        grad_k_prompt[:, columns] = slab[:SLAB, :].astype(BF16)
+        grad_v_prompt[:, columns] = slab[SLAB:, :].astype(BF16)
 
     for i in range(1, HEADS):
         slab_link(i).wait_send()
         slab_back(i).wait_send()
-    for d in range(1, SPAN + 1):
+    for d in (2, 4):
         resp_link(d).wait_send()
         resp_back(d).wait_send()
+    for d in (1, 3):
+        core_resp_link(d).wait_send()
+        core_resp_back(d).wait_send()
     for chip in PLACE:
         core_link(chip).wait_send()
         core_back(chip).wait_send()
@@ -442,12 +478,21 @@
     x_back().wait_send()
 
 
+def write_out(*refs):
+    sems = refs[12]
+    copies = [pltpu.make_async_copy(refs[i], refs[6 + i], sems.at[i]) for i in range(6)]
+    for copy in copies:
+        copy.start()
+    for copy in copies:
+        copy.wait()
+
+
 def shards(prompt_k, prompt_v, resp_q, resp_k, resp_v, grad_out, resp_lengths):
     vmem = pl.BlockSpec(memory_space=pltpu.VMEM)
     anywhere = pl.BlockSpec(memory_space=pl.ANY)
-    links = 2 * (HEADS - 1) + 2 * SPAN + 2 * (6 + 1 + 8)
+    links = 2 * (HEADS - 1) + 2 * 4 + 2 * (6 + 1 + 8)
     like = jax.ShapeDtypeStruct
-    return pl.pallas_call(
+    results = pl.pallas_call(
         kernel,
         out_shape=(
             like((ROWS, GROUP * HD), BF16),
@@ -467,27 +512,27 @@
             pltpu.VMEM((HD + 16, KEYS), BF16),
             pltpu.VMEM((GROUP, HD, ROWS), BF16),
             pltpu.VMEM((GROUP * ROWS, HD), BF16),
-            pltpu.VMEM((GROUP, HD, ROWS), F32),
             pltpu.VMEM((GROUP, 2 * HD, ROWS), BF16),
             pltpu.VMEM((GROUP * ROWS, HD), BF16),
             pltpu.VMEM((KEYS, GROUP * ROWS), BF16),
+            pltpu.VMEM((CHUNK, GROUP * ROWS), BF16),
             pltpu.VMEM((CHUNK, ROWS), F32),
             pltpu.VMEM((CHUNK, ROWS), F32),
             pltpu.VMEM((CHUNK, ROWS), F32),
             pltpu.VMEM((GROUP, ROWS), F32),
             pltpu.VMEM((CHUNKS, GROUP, ROWS), F32),
             pltpu.VMEM((GROUP, HD + 16, ROWS), F32),
-            pltpu.VMEM((GROUP, ROWS), F32),
-            pltpu.VMEM((HEADS, 2, SLAB, HD), F32),
-            pltpu.VMEM((HEADS, 2, SLAB, HD), F32),
+            pltpu.VMEM((HEADS, 2 * SLAB, HD), BF16),
+            pltpu.VMEM((HEADS, 2 * SLAB, HD), BF16),
             pltpu.VMEM((2, KEYS, HD), BF16),
             pltpu.VMEM((2, 8 * BLOCK, HD), BF16),
             pltpu.VMEM((2, 3, 2, BLOCK, HD), BF16),
             pltpu.VMEM((2, BLOCK, HD), BF16),
             pltpu.VMEM((2, BLOCK, HD), BF16),
-            pltpu.VMEM((SPAN, 2, ROWS, HD), BF16),
-            pltpu.VMEM((HEADS, 2, SLAB, HD), F32),
-            pltpu.VMEM((HEADS, 2, SLAB, HD), F32),
+            pltpu.VMEM((2, 2, ROWS, HD), BF16),
+            pltpu.VMEM((2, 2, ROWS, HD), BF16),
+            pltpu.VMEM((HEADS, 2 * SLAB, HD), BF16),
+            pltpu.VMEM((HEADS, 2 * SLAB, HD), BF16),
             pltpu.SemaphoreType.DMA((4,)),
             pltpu.SemaphoreType.DMA((links,)),
             pltpu.SemaphoreType.DMA((links,)),
@@ -502,6 +547,14 @@
         ),
         name="shared_prompt_attention",
     )(resp_lengths, prompt_k, prompt_v, resp_q, resp_k, resp_v, grad_out)
+    return pl.pallas_call(
+        write_out,
+        out_shape=tuple(like(r.shape, r.dtype) for r in results),
+        in_specs=[vmem] * 6,
+        out_specs=[anywhere] * 6,
+        scratch_shapes=[pltpu.SemaphoreType.DMA((6,))],
+        name="write_out",
+    )(*results)
 
 
 def solution(mesh):

time: 129 us -> 94.6 us (0.73)
  Pallas kernels: 122 us -> 93.6 us
  local copies, waits for them, and re-layouts: 6.11 us -> 0 us
    pallas_call x1, Pallas kernels: 122 us -> 91.3 us  [shards(): pl.pallas_call(kernel, out_shape=(like((ROWS, GROUP * HD), BF16), like((R...]
    unnamed x16 -> x0, local copies, waits for them, and re-layouts: 6.11 us -> none
    pallas_call x0 -> x1, Pallas kernels: none -> 2.37 us  [shards(): pl.pallas_call(write_out, out_shape=tuple((like(r.shape, r.dtype) for r i...]
where the time goes in v2:
time: 94.6 us; the launch traced here: 94.5 us
  Pallas kernels  93.6 us (99%)
    pallas_call x1, Pallas kernels, shards(): pl.pallas_call(kernel, out_shape=(like((ROWS, GROUP * HD), BF16), like((R...  91.3 us
    pallas_call x1, Pallas kernels, shards(): pl.pallas_call(write_out, out_shape=tuple((like(r.shape, r.dtype) for r i...  2.37 us

profile of v2, /device:TPU:2, one launch (start us, length us, event | category | flops | bytes accessed | tf_op | source)
XLA Modules:
  0.0 94.5 jit_solution(7611590764769524381)
XLA Ops:
  0.6 91.3 %shared_prompt_attention.1 = (bf16[256,1024]{1,0:T(8,128)(2,1)}, bf16[256,1024]{1,0:T(8,128)(2,1)}, bf16[256,128]{1,0:T(8,128)(2,1)}, bf16[256,128]{1,0:T(8,128)...) custom-call(s32[8]{0:T(128)} %lengths.1, bf16[40,1024]{1,0:T(8,128)(2,1)} %prompt_k.1, ...), custom_call_target="tpu_custom_call" | custom-call | flops 20132659200 | bytes 4194304 | tf_op jit(solution)/shard_map/shared_prompt_attention/pallas_call | solution.py:495
  91.9 2.4 %write_out.1 = (bf16[256,1024]{1,0:T(8,128)(2,1)}, bf16[256,1024]{1,0:T(8,128)(2,1)}, bf16[256,128]{1,0:T(8,128)(2,1)}, bf16[256,128]{1,0:T(8,128)(2,1)}, bf16[4...) custom-call(bf16[256,1024]{1,0:T(8,128)(2,1)} %get-tuple-element.12.refs_0_, bf16[256,1024]{1,0:T(8,128)(2,1)} %get-tuple-element.13.refs_1_, ...), custom_call_target="tpu_custom_call" | custom-call | tf_op jit(solution)/shard_map/write_out/pallas_call | solution.py:550

commit v3 on v2

--- a/solution.py
+++ b/solution.py
@@ -15,6 +15,7 @@
 SPAN = 4
 BLOCK = 320
 SLAB = 40
+WIDE = 4
 CHUNK = 1280
 CHUNKS = 5
 KEYS = CHUNK * CHUNKS
@@ -53,8 +54,6 @@
     grad_v_resp,
     grad_k_prompt,
     grad_v_prompt,
-    q_in,
-    cot_in,
     kv,
     k_cols,
     v_cols,
@@ -64,9 +63,7 @@
     cot_rows,
     weights,
     scaled,
-    wide_a,
-    wide_b,
-    mask,
+    wide,
     run_max,
     chunk_max,
     acc,
@@ -76,7 +73,6 @@
     from_core,
     from_y,
     from_x,
-    to_x,
     from_resp,
     from_core_resp,
     back_out,
@@ -153,7 +149,8 @@
         )
 
     def x_back():
-        return link(("x_back",), to_x, from_x, at(1, 0, 0))
+        sums = partial.at[:, pl.ds(PLACE[(1, 0)], BLOCK), :]
+        return link(("x_back",), sums, from_x, at(1, 0, 0))
 
     def core_resp_back(d):
         return link(
@@ -180,9 +177,15 @@
         pltpu.make_async_copy(
             resp_v_hbm, kv.at[1, pl.ds(SPAN * ROWS, ROWS), :], local_sem.at[1]
         ),
-        pltpu.make_async_copy(q_hbm, q_in, local_sem.at[2]),
-        pltpu.make_async_copy(cot_hbm, cot_in, local_sem.at[3]),
     ]
+    for g in range(GROUP):
+        columns, rows = pl.ds(g * HD, HD), pl.ds(g * ROWS, ROWS)
+        for i, (array, by_head) in enumerate(((q_hbm, q_rows), (cot_hbm, cot_rows))):
+            loads.append(
+                pltpu.make_async_copy(
+                    array.at[:, columns], by_head.at[rows, :], local_sem.at[2 + 2 * g + i]
+                )
+            )
     for load in loads:
         load.start()
     barrier = pltpu.get_barrier_semaphore()
@@ -198,19 +201,21 @@
     pl.semaphore_wait(barrier, len(partners))
     for i in range(1, HEADS):
         slab_link(i).start()
+
     loads[0].wait()
     loads[1].wait()
     for d in (4, 2):
-        resp_link(d).start()
-
-    loads[2].wait()
-    loads[3].wait()
+
+        @pl.when(seq + d < 16)
+        def _():
+            resp_link(d).start()
+
+    for load in loads[2:]:
+        load.wait()
     for g in range(GROUP):
-        columns = slice(g * HD, (g + 1) * HD)
-        q_rows[g * ROWS : (g + 1) * ROWS, :] = q_in[:, columns]
-        q_cols[g] = q_in[:, columns].T
-        cot_rows[g * ROWS : (g + 1) * ROWS, :] = cot_in[:, columns]
-        cot_cols[g, :HD, :] = cot_in[:, columns].T
+        rows = slice(g * ROWS, (g + 1) * ROWS)
+        q_cols[g] = q_rows[rows, :].T
+        cot_cols[g, :HD, :] = cot_rows[rows, :].T
         cot_cols[g, HD:, :] = jnp.zeros((HD, ROWS), BF16)
     token = first_row + lax.broadcasted_iota(jnp.int32, (1, ROWS), 1)
     start = jnp.zeros((1, ROWS), jnp.int32)
@@ -219,10 +224,11 @@
         end = end + lengths[i]
         start = jnp.where(token >= end, end, start)
     key = first_row - SPAN * ROWS + lax.broadcasted_iota(jnp.int32, (CHUNK, ROWS), 0)
-    mask[...] = jnp.where((key >= start) & (key <= token), 0.0, MASKED)
+    allowed = (key >= start) & (key <= token)
+    scaled[:, :ROWS] = jnp.where(allowed, 0.0, MASKED).astype(BF16)
     run_max[...] = jnp.full_like(run_max, MASKED)
     acc[...] = jnp.zeros_like(acc)
-    ones_row = lax.broadcasted_iota(jnp.int32, (16, KEYS), 0) == 0
+    ones_row = lax.broadcasted_iota(jnp.int32, (16, CHUNK), 0) == 0
     v_cols[HD:, :] = jnp.where(ones_row, 1.0, 0.0).astype(BF16)
 
     for i in range(1, HEADS):
@@ -240,82 +246,93 @@
 
     def turn(chunk):
         rows = key_rows(chunk)
-        v_cols[:HD, rows] = kv[1, rows, :].T
-
-    def forward(chunk, masked, middle=None):
+        v_cols[:HD, :] = kv[1, rows, :].T
+
+    def forward(chunk, masked, middle):
         rows = key_rows(chunk)
-        wide = (wide_a, wide_b)
 
         def scores(g):
             s = dot(kv[0, rows, :], q_cols[g])
             if masked:
-                s = s + mask[...]
-            wide[g % 2][...] = s
+                s = s + scaled[:, :ROWS].astype(F32)
+            wide[g % WIDE] = s
             earlier = run_max[g : g + 1, :]
             largest = jnp.maximum(earlier, jnp.max(s, axis=0, keepdims=True))
             run_max[g : g + 1, :] = largest
             chunk_max[chunk, g : g + 1, :] = largest
-            return largest, jnp.exp2((earlier - largest) * EXP2_SCALE)
+            return jnp.exp2((earlier - largest) * EXP2_SCALE)
 
         def output(g, shrink):
-            part = dot(v_cols[:, rows], weights[rows, g * ROWS : (g + 1) * ROWS])
-            acc[g] = acc[g] * shrink + part
-
-        largest, shrink = scores(0)
-        last = None
-        for g in range(GROUP):
-            if g + 1 < GROUP:
-                following = scores(g + 1)
-            w = jnp.exp2((wide[g % 2][...] - largest) * EXP2_SCALE)
-            weights[rows, g * ROWS : (g + 1) * ROWS] = w.astype(BF16)
-            if last is not None:
-                output(g - 1, last)
-            last = shrink
-            if middle is not None and g == GROUP // 2:
-                middle()
-            if g + 1 < GROUP:
-                largest, shrink = following
-        output(GROUP - 1, last)
-
-    for d in (2, 4):
-        resp_link(d).wait_recv()
-    for d in (1, 3):
-        core_resp_link(d).start()
-
-    def pass_on():
-        x_link().wait_recv()
-        for dy in (1, 3, 2):
-            y_link(1, dy).start()
-        core_link((1, 0)).start()
-        for dy in (1, 3):
-            y_link(0, dy).wait_recv()
-            core_link((0, dy)).start()
+            columns = slice(g * ROWS, (g + 1) * ROWS)
+            largest = chunk_max[chunk, g : g + 1, :]
+            w = jnp.exp2((wide[g % WIDE] - largest) * EXP2_SCALE).astype(BF16)
+            weights[rows, columns] = w
+            acc[g] = acc[g] * shrink + dot(v_cols[...], weights[rows, columns])
+
+        for first in range(0, GROUP, WIDE):
+            some = range(first, first + WIDE)
+            shrinks = [scores(g) for g in some]
+            middle(first // WIDE)
+
+            @pl.when(seq >= 0)
+            def _():
+                for g, shrink in zip(some, shrinks):
+                    output(g, shrink)
+
+    def during_near(half):
+        if half == 0:
+            y_link(0, 3).wait_recv()
+            core_link((0, 3)).start()
+            core_link((1, 0)).start()
+        else:
+            y_link(0, 2).wait_recv()
+            core_link((0, 2)).start()
+
+    def during_far(half):
+        if half == 1:
+            for d in (2, 4):
+
+                @pl.when(seq >= d)
+                def _():
+                    resp_link(d).wait_recv()
+
+                @pl.when(seq < d)
+                def _():
+                    first = (SPAN - d) * ROWS
+                    kv[:, first : first + ROWS, :] = jnp.zeros((2, ROWS, HD), BF16)
+
+            for d in (1, 3):
+                core_resp_link(d).start()
+
+    def during_resp(half):
+        if half == 0:
+            for dy in (1, 3):
+                y_link(1, dy).wait_recv()
+                core_link((1, dy)).start()
+
+    y_link(0, 1).wait_recv()
+    core_link((0, 1)).start()
+    x_link().wait_recv()
+    for dy in (1, 3, 2):
+        y_link(1, dy).start()
+    core_link((0, 0)).wait_recv()
+    core_link((0, 1)).wait_recv()
+    turn(1)
+    forward(1, False, during_near)
+
+    core_link((0, 3)).wait_recv()
+    core_link((0, 2)).wait_recv()
+    turn(2)
+    forward(2, False, during_far)
 
     for d in (1, 3):
         core_resp_link(d).wait_recv()
     turn(0)
-    forward(0, True, pass_on)
+    forward(0, True, during_resp)
 
     def prompt_chunk(chunk, carry):
-        @pl.when(chunk == 1)
-        def _():
-            y_link(0, 2).wait_recv()
-            core_link((0, 2)).start()
-            core_link((0, 0)).wait_recv()
-            core_link((0, 1)).wait_recv()
-
-        @pl.when(chunk == 2)
-        def _():
-            for dy in (1, 3):
-                y_link(1, dy).wait_recv()
-                core_link((1, dy)).start()
-            core_link((0, 3)).wait_recv()
-            core_link((0, 2)).wait_recv()
-
         @pl.when(chunk == 3)
         def _():
-            y_link(1, 2).wait_recv()
-            core_link((1, 2)).start()
             core_link((1, 0)).wait_recv()
             core_link((1, 1)).wait_recv()
 
@@ -324,16 +341,24 @@
             core_link((1, 3)).wait_recv()
             core_link((1, 2)).wait_recv()
 
+        def during(half):
+            if half == 0:
+
+                @pl.when(chunk == 3)
+                def _():
+                    y_link(1, 2).wait_recv()
+                    core_link((1, 2)).start()
+
         turn(chunk)
-        forward(chunk, False)
+        forward(chunk, False, during)
         return carry
 
-    lax.fori_loop(1, CHUNKS, prompt_chunk, 0)
+    lax.fori_loop(3, CHUNKS, prompt_chunk, 0)
 
     for g in range(GROUP):
         inverse = 1.0 / acc[g, HD : HD + 1, :]
         rounded = (acc[g, :HD, :] * inverse).astype(BF16)
-        out_ref[:, g * HD : (g + 1) * HD] = rounded.T
+        scaled[:ROWS, g * HD : (g + 1) * HD] = rounded.T
         products = cot_cols[g, :HD, :].astype(F32) * rounded.astype(F32)
         rest = -jnp.sum(products, axis=0, keepdims=True)
         for i in range(3):
@@ -345,6 +370,10 @@
                 (chunk_max[chunk, g : g + 1, :] - run_max[g : g + 1, :]) * EXP2_SCALE
             )
 
+    out_copy = pltpu.make_async_copy(
+        scaled.at[pl.ds(0, ROWS), pl.ds(0, GROUP * HD)], out_ref, local_sem.at[2 + 2 * GROUP]
+    )
+    out_copy.start()
     is_one = lax.broadcasted_iota(jnp.int32, (CHUNK, HD), 1) < 3
     ones_columns = jnp.where(is_one, 1.0, 0.0).astype(BF16)
 
@@ -363,39 +392,39 @@
         for dy in (1, 2, 3):
             y_back(1, dy).wait_recv()
             total = total + from_y[1, dy - 1].astype(F32)
-        to_x[...] = total.astype(BF16)
+        partial[:, place : place + BLOCK, :] = total.astype(BF16)
         x_back().start()
 
-    def backward(step, carry):
-        chunk = CHUNKS - 1 - step
+    def backward(chunk, middle=None):
         rows = key_rows(chunk)
         k_cols[:, rows] = kv[0, rows, :].T
         values = jnp.concatenate([kv[1, rows, :], ones_columns], axis=1)
-        wide = (wide_a, wide_b)
-        wide[0][...] = dot(values, cot_cols[0])
         for g in range(GROUP):
-            if g + 1 < GROUP:
-                wide[(g + 1) % 2][...] = dot(values, cot_cols[g + 1])
             columns = slice(g * ROWS, (g + 1) * ROWS)
+            wide[g % WIDE] = dot(values, cot_cols[g])
             w = weights[rows, columns].astype(F32) * chunk_max[chunk, g : g + 1, :]
             scaled[:, columns] = w.astype(BF16)
-            weights[rows, columns] = (w * wide[g % 2][...]).astype(BF16)
-        for earlier in (4, 3, 2, 1):
-
-            @pl.when(chunk == earlier - 1)
-            def _():
-                for chip in CHIPS[earlier]:
-                    pair_sum(chip)
-                    if chip[1] != 0:
-                        y_back(*chip).start()
-
+            weights[rows, columns] = (w * wide[g % WIDE]).astype(BF16)
+        if middle is not None:
+            middle()
         partial[1, rows, :] = dot(scaled[...], cot_rows[...]).astype(BF16)
         partial[0, rows, :] = (dot(weights[rows, :], q_rows[...]) * SCALE).astype(BF16)
 
-        @pl.when(chunk == 0)
-        def _():
-            sum_over_y()
-
+    def pass_back(chunk):
+        for chip in CHIPS[chunk]:
+            pair_sum(chip)
+            if chip[1] != 0:
+                y_back(*chip).start()
+
+    def prompt_back(step, carry):
+        chunk = CHUNKS - 1 - step
+        for later in (1, 2):
+
+            @pl.when(chunk == later)
+            def _():
+                pass_back(later + 2)
+
+        backward(chunk)
         for done in (4, 3, 2, 1):
 
             @pl.when(chunk == done)
@@ -405,7 +434,17 @@
 
         return carry
 
-    lax.fori_loop(0, CHUNKS, backward, 0)
+    out_copy.wait()
+    lax.fori_loop(0, CHUNKS - 1, prompt_back, 0)
+    pass_back(2)
+
+    def last_sums():
+        @pl.when(seq >= 0)
+        def _():
+            pass_back(1)
+            sum_over_y()
+
+    backward(0, last_sums)
 
     for d in (1, 3):
         core_resp_back(d).start()
@@ -423,7 +462,10 @@
         total = partial[:, near, :].astype(F32) + from_core_resp[d // 2].astype(F32)
         partial[:, near, :] = total.astype(BF16)
     for d in (4, 2):
-        resp_back(d).start()
+
+        @pl.when(seq >= d)
+        def _():
+            resp_back(d).start()
 
     for g in range(2, 6):
         grad_query(g)
@@ -445,7 +487,15 @@
 
     total = partial[:, SPAN * ROWS : CHUNK, :].astype(F32)
     for d in (2, 4):
-        resp_back(d).wait_recv()
+
+        @pl.when(seq + d < 16)
+        def _():
+            resp_back(d).wait_recv()
+
+        @pl.when(seq + d >= 16)
+        def _():
+            from_resp[d // 2 - 1] = jnp.zeros((2, ROWS, HD), BF16)
+
         total = total + from_resp[d // 2 - 1].astype(F32)
     grad_k_resp[...] = total[0].astype(BF16)
     grad_v_resp[...] = total[1].astype(BF16)
@@ -463,8 +513,15 @@
         slab_link(i).wait_send()
         slab_back(i).wait_send()
     for d in (2, 4):
-        resp_link(d).wait_send()
-        resp_back(d).wait_send()
+
+        @pl.when(seq + d < 16)
+        def _():
+            resp_link(d).wait_send()
+
+        @pl.when(seq >= d)
+        def _():
+            resp_back(d).wait_send()
+
     for d in (1, 3):
         core_resp_link(d).wait_send()
         core_resp_back(d).wait_send()
@@ -503,22 +560,18 @@
             like((SLAB, HEADS * HD), BF16),
         ),
         in_specs=[pl.BlockSpec(memory_space=pltpu.SMEM), vmem, vmem] + [anywhere] * 4,
-        out_specs=[vmem] * 6,
+        out_specs=[anywhere] + [vmem] * 5,
         scratch_shapes=[
-            pltpu.VMEM((ROWS, GROUP * HD), BF16),
-            pltpu.VMEM((ROWS, GROUP * HD), BF16),
             pltpu.VMEM((2, KEYS, HD), BF16),
             pltpu.VMEM((HD, KEYS), BF16),
-            pltpu.VMEM((HD + 16, KEYS), BF16),
+            pltpu.VMEM((HD + 16, CHUNK), BF16),
             pltpu.VMEM((GROUP, HD, ROWS), BF16),
             pltpu.VMEM((GROUP * ROWS, HD), BF16),
             pltpu.VMEM((GROUP, 2 * HD, ROWS), BF16),
             pltpu.VMEM((GROUP * ROWS, HD), BF16),
             pltpu.VMEM((KEYS, GROUP * ROWS), BF16),
             pltpu.VMEM((CHUNK, GROUP * ROWS), BF16),
-            pltpu.VMEM((CHUNK, ROWS), F32),
-            pltpu.VMEM((CHUNK, ROWS), F32),
-            pltpu.VMEM((CHUNK, ROWS), F32),
+            pltpu.VMEM((WIDE, CHUNK, ROWS), F32),
             pltpu.VMEM((GROUP, ROWS), F32),
             pltpu.VMEM((CHUNKS, GROUP, ROWS), F32),
             pltpu.VMEM((GROUP, HD + 16, ROWS), F32),
@@ -528,17 +581,16 @@
             pltpu.VMEM((2, 8 * BLOCK, HD), BF16),
             pltpu.VMEM((2, 3, 2, BLOCK, HD), BF16),
             pltpu.VMEM((2, BLOCK, HD), BF16),
-            pltpu.VMEM((2, BLOCK, HD), BF16),
             pltpu.VMEM((2, 2, ROWS, HD), BF16),
             pltpu.VMEM((2, 2, ROWS, HD), BF16),
             pltpu.VMEM((HEADS, 2 * SLAB, HD), BF16),
             pltpu.VMEM((HEADS, 2 * SLAB, HD), BF16),
-            pltpu.SemaphoreType.DMA((4,)),
+            pltpu.SemaphoreType.DMA((3 + 2 * GROUP,)),
             pltpu.SemaphoreType.DMA((links,)),
             pltpu.SemaphoreType.DMA((links,)),
         ],
         compiler_params=pltpu.CompilerParams(
-            collective_id=0, has_side_effects=True, vmem_limit_bytes=60 * 2**20
+            collective_id=0, has_side_effects=True, vmem_limit_bytes=63 * 2**20
         ),
         cost_estimate=pl.CostEstimate(
             flops=12 * ROWS * GROUP * KEYS * HD,

time: 94.6 us -> 89.2 us (0.943)
  the two profiles are of different devices: /device:TPU:2 before, /device:TPU:6 now
where the time goes in v3:
time: 89.2 us; the launch traced here: 89 us
  Pallas kernels  88.2 us (99%)
    pallas_call x1, Pallas kernels, shards(): pl.pallas_call(kernel, out_shape=(like((ROWS, GROUP * HD), BF16), like((R...  85.8 us
    pallas_call x1, Pallas kernels, shards(): pl.pallas_call(write_out, out_shape=tuple((like(r.shape, r.dtype) for r i...  2.37 us

profile of v3, /device:TPU:6, one launch (start us, length us, event | category | flops | bytes accessed | tf_op | source)
XLA Modules:
  0.0 89.0 jit_solution(7980890471129344699)
XLA Ops:
  0.6 85.8 %shared_prompt_attention.1 = (bf16[256,1024]{1,0:T(8,128)(2,1)}, bf16[256,1024]{1,0:T(8,128)(2,1)}, bf16[256,128]{1,0:T(8,128)(2,1)}, bf16[256,128]{1,0:T(8,128)...) custom-call(s32[8]{0:T(128)} %lengths.1, bf16[40,1024]{1,0:T(8,128)(2,1)} %prompt_k.1, ...), custom_call_target="tpu_custom_call" | custom-call | flops 20132659200 | bytes 4194304 | tf_op jit(solution)/shard_map/shared_prompt_attention/pallas_call | solution.py:552
  86.5 2.4 %write_out.1 = (bf16[256,1024]{1,0:T(8,128)(2,1)}, bf16[256,1024]{1,0:T(8,128)(2,1)}, bf16[256,128]{1,0:T(8,128)(2,1)}, bf16[256,128]{1,0:T(8,128)(2,1)}, bf16[4...) custom-call(bf16[256,1024]{1,0:T(8,128)(2,1)} %get-tuple-element.12.refs_0_, bf16[256,1024]{1,0:T(8,128)(2,1)} %get-tuple-element.13.refs_1_, ...), custom_call_target="tpu_custom_call" | custom-call | tf_op jit(solution)/shard_map/write_out/pallas_call | solution.py:602

commit v4 on v3

--- a/solution.py
+++ b/solution.py
@@ -381,10 +381,9 @@
         core_back(chip).wait_recv()
         row = PLACE[chip]
         half = (row - CHUNK) // 2
-        mine = partial[:, row : row + BLOCK, :].astype(F32)
         partial[:, row : row + BLOCK, :] = (
-            mine + from_core[:, half : half + BLOCK, :].astype(F32)
-        ).astype(BF16)
+            partial[:, row : row + BLOCK, :] + from_core[:, half : half + BLOCK, :]
+        )
 
     def sum_over_y():
         place = PLACE[(1, 0)]
@@ -459,8 +458,7 @@
     for d in (1, 3):
         core_resp_back(d).wait_recv()
         near = pl.ds(pl.multiple_of((SPAN - (2 * core + d - 1)) * ROWS, ROWS), ROWS)
-        total = partial[:, near, :].astype(F32) + from_core_resp[d // 2].astype(F32)
-        partial[:, near, :] = total.astype(BF16)
+        partial[:, near, :] = partial[:, near, :] + from_core_resp[d // 2]
     for d in (4, 2):
 
         @pl.when(seq >= d)
@@ -536,12 +534,16 @@
 
 
 def write_out(*refs):
-    sems = refs[12]
-    copies = [pltpu.make_async_copy(refs[i], refs[6 + i], sems.at[i]) for i in range(6)]
-    for copy in copies:
-        copy.start()
-    for copy in copies:
-        copy.wait()
+    sources, targets, held, sems = refs[:6], refs[6:12], refs[12:18], refs[18]
+    loads = [pltpu.make_async_copy(sources[i], held[i], sems.at[i]) for i in range(6)]
+    stores = [pltpu.make_async_copy(held[i], targets[i], sems.at[6 + i]) for i in range(6)]
+    for load in loads:
+        load.start()
+    for load, store in zip(loads, stores):
+        load.wait()
+        store.start()
+    for store in stores:
+        store.wait()
 
 
 def shards(prompt_k, prompt_v, resp_q, resp_k, resp_v, grad_out, resp_lengths):
@@ -602,9 +604,10 @@
     return pl.pallas_call(
         write_out,
         out_shape=tuple(like(r.shape, r.dtype) for r in results),
-        in_specs=[vmem] * 6,
+        in_specs=[anywhere] * 6,
         out_specs=[anywhere] * 6,
-        scratch_shapes=[pltpu.SemaphoreType.DMA((6,))],
+        scratch_shapes=[pltpu.VMEM(r.shape, r.dtype) for r in results]
+        + [pltpu.SemaphoreType.DMA((12,))],
         name="write_out",
     )(*results)
 

time: 89.2 us -> 89 us (level)
  no operation moved by 1% of the time
where the time goes in v4:
time: 89 us; the launch traced here: 88.8 us
  Pallas kernels  88 us (99%)
    pallas_call x1, Pallas kernels, shards(): pl.pallas_call(kernel, out_shape=(like((ROWS, GROUP * HD), BF16), like((R...  85.8 us
    pallas_call x1, Pallas kernels, shards(): pl.pallas_call(write_out, out_shape=tuple((like(r.shape, r.dtype) for r i...  2.2 us

profile of v4, /device:TPU:6, one launch (start us, length us, event | category | flops | bytes accessed | tf_op | source)
XLA Modules:
  0.0 88.8 jit_solution(2930221667844532226)
XLA Ops:
  0.6 85.8 %shared_prompt_attention.1 = (bf16[256,1024]{1,0:T(8,128)(2,1)}, bf16[256,1024]{1,0:T(8,128)(2,1)}, bf16[256,128]{1,0:T(8,128)(2,1)}, bf16[256,128]{1,0:T(8,128)...) custom-call(s32[8]{0:T(128)} %lengths.1, bf16[40,1024]{1,0:T(8,128)(2,1)} %prompt_k.1, ...), custom_call_target="tpu_custom_call" | custom-call | flops 20132659200 | bytes 4194304 | tf_op jit(solution)/shard_map/shared_prompt_attention/pallas_call | solution.py:554
  86.4 2.2 %write_out.1 = (bf16[256,1024]{1,0:T(8,128)(2,1)}, bf16[256,1024]{1,0:T(8,128)(2,1)}, bf16[256,128]{1,0:T(8,128)(2,1)}, bf16[256,128]{1,0:T(8,128)(2,1)}, bf16[4...) custom-call(bf16[256,1024]{1,0:T(8,128)(2,1)} %get-tuple-element.12.refs_0_, bf16[256,1024]{1,0:T(8,128)(2,1)} %get-tuple-element.13.refs_1_, ...), custom_call_target="tpu_custom_call" | custom-call | tf_op jit(solution)/shard_map/write_out/pallas_call | solution.py:604
